TPU v7x, 32 devices: a whole 2x2x4 slice. The times are simulated.
32 devices in a mesh: row: 4 (over y, x), col: 8 (over z, core).
Axes of the slice: x: 2, y: 2, z: 4, core: 2. Of those that a mesh axis runs over, the one named last changes fastest.
Arguments:
- landmarks: float32 [20480, 128], P(('row', 'col')), may hold values from -6 to 6
- slab_points: float32 [2048, 128], P('col'), may hold values from -6 to 6
- panel_points: float32 [2, 256, 128], replicated, may hold values from -6 to 6, as said below
- inverse_blocks: float32 [2, 256, 256], replicated, as said below
Outputs:
- updated_slab: float32 [20480, 2048], P('row', 'col')
Inputs may be any that keep to these rules, and one draw needn't show every extreme that they name: `panel_points`: points of order one, at most 6 in magnitude. inverse_blocks[0] is the inverse of the lower Cholesky factor of gaussian(panel_points[0], panel_points[0]) + 0.001 I; inverse_blocks[1] is the inverse of the lower Cholesky factor of gaussian(panel_points[1], panel_points[1]) - first_next first_next^T + 0.001 I. Both are lower triangular with a positive diagonal.
All inputs are finite; a program needn't handle non-finite values.
Results may differ from a plain program's by a relative error of at most 0.0003.
Values sent between devices are 32-bit elements; how exact they have to be, the bound alone decides.
No kernel may reach another device: no remote copies, remote signals or barrier semaphores. Data moves between devices by JAX's collectives and lax.ppermute only.
A program may use at most 128 MiB of HBM per device.

v0:
```python
import jax
import jax.numpy as jnp
from jax import lax
from jax.sharding import PartitionSpec as P


def passed_along(shard, axis, by):
    size = lax.axis_size(axis)
    return lax.ppermute(shard, axis, [(i, (i + by) % size) for i in range(size)])


def dot_rows(left_matrix, right_matrix):
    return lax.dot_general(
        left_matrix,
        right_matrix,
        (((1,), (1,)), ((), ())),
        precision=lax.Precision.HIGHEST,
        preferred_element_type=jnp.float32,
    )


def gaussian(left_points, right_points):
    inner = dot_rows(left_points, right_points)
    left_norms = jnp.sum(left_points * left_points, axis=1)[:, None]
    right_norms = jnp.sum(right_points * right_points, axis=1)[None, :]
    return jnp.exp((2.0 * inner - left_norms - right_norms) / left_points.shape[1])


def factors(points, panel_points, inverse_blocks, first_next):
    first_panel = dot_rows(gaussian(points, panel_points[0]), inverse_blocks[0])
    second_raw = gaussian(points, panel_points[1]) - dot_rows(first_panel, first_next)
    second_panel = dot_rows(second_raw, inverse_blocks[1])
    return jnp.concatenate([first_panel, second_panel], axis=1)


def local(landmarks, slab_points, panel_points, inverse_blocks):
    first_next = dot_rows(gaussian(panel_points[1], panel_points[0]), inverse_blocks[0])
    slab_factors = factors(slab_points, panel_points, inverse_blocks, first_next)
    col_count = lax.axis_size("col")
    block_rows = landmarks.shape[0]
    col_index = lax.axis_index("col")
    row_factors = lax.all_gather(
        factors(landmarks, panel_points, inverse_blocks, first_next), "col", axis=0, tiled=True
    )

    def block_result(landmark_block, row_start):
        factor_rows = lax.dynamic_slice_in_dim(row_factors, row_start, landmark_block.shape[0], 0)
        return gaussian(landmark_block, slab_points) - dot_rows(factor_rows, slab_factors)

    def place_block(running, landmark_block, row_start):
        return lax.dynamic_update_slice_in_dim(
            running, block_result(landmark_block, row_start), row_start, 0
        )

    zero_tile = jnp.zeros((block_rows * col_count, slab_points.shape[0]), jnp.float32)
    result = place_block(zero_tile, landmarks, col_index * block_rows)

    def advance(section_index, carried):
        running, held_block = carried
        held_block = passed_along(held_block, "col", 1)
        row_start = (col_index - section_index) % col_count * block_rows
        return (place_block(running, held_block, row_start), held_block)

    result, held_last = lax.fori_loop(1, col_count, advance, (result, landmarks))
    return result


def solution(mesh):
    in_specs = (P(("row", "col"), None), P("col", None), P(), P())
    out_specs = P("row", "col")
    return jax.shard_map(local, mesh=mesh, in_specs=in_specs, out_specs=out_specs, check_vma=False)
```

profile of v0, /device:TPU:0, one launch (start us, length us, event | category | flops | bytes accessed | tf_op | source)
XLA Modules:
  0.0 230.1 jit_solution(16922470395194710319)
XLA Ops:
  8.9 1.6 fusion.28
  10.5 1.6 fusion.24
  12.2 1.4 fusion.40
  13.6 1.8 fusion.53
  15.8 1.2 convolution_subtract_fusion
  17.9 1.1 pad_maximum_fusion
  22.5 98.9 %all-gather.2.cloned.1.call-done = f32[5120,512]{0,1:T(8,128)} async-done(((f32[640,512]{0,1:T(8,128)}), f32[5120,512]{0,1:T(8,128)}) %all-gather.2.cloned.1.call-update) | async-done | bytes 10485776 | tf_op jit(solution)/shard_map/all_gather | solution.py:42
  121.7 3.5 %fusion.18 = f32[5120,256]{1,0:T(8,128)S(1)} fusion(f32[5120,256]{1,0:T(8,128)S(1)} %broadcast_in_dim.6, s32[]{:T(128)S(6)} %select_n.35, f32[640,256]{1,0:T(8,128)S(1)} %fusion.32, f32[5120,512]{0,1:T(8,128)} %all-gather.2.cloned.1.call-done, f32[256,256]{0,1:T(8,128)S(1)} %fusion.45, f32[256,256]{0,1:T(8,128)S(1)} %fusion.49), kind=kOutput, calls=%fused_computation.16 | convolution fusion | flops 1006927872 | bytes 3146752 | tf_op jit(solution)/shard_map/dot_general | solution.py:13
  125.2 2.3 %copy-done.1 = f32[5120,256]{1,0:T(8,128)} copy-done((f32[5120,256]{1,0:T(8,128)}, f32[5120,256]{1,0:T(8,128)S(1)}, u32[]{:S(2)}) %copy-start.1) | copy-done | bytes 5242904
  127.6 95.7 %while.17 = (s32[]{:T(128)}, f32[5120,256]{1,0:T(8,128)}, f32[640,128]{1,0:T(8,128)S(1)}, f32[256,128]{1,0:T(8,128)S(1)}, f32[256]{0:T(256)S(1)}, /*index=5*/s32...) while((s32[]{:T(128)}, f32[5120,256]{1,0:T(8,128)}, ...), condition=%wide.region_6.0_spmd, body=%wide.region_4.6_spmd.sunk | while | flops 1259273600 | bytes 6561108 | solution.py:64
  127.8 8.0 %collective-permute-done = f32[640,128]{1,0:T(8,128)S(1)} collective-permute-done((f32[640,128]{1,0:T(8,128)S(1)}, f32[640,128]{1,0:T(8,128)S(1)}, u32[]{:S(2)}, u32[]{:S(2)}) %collective-permute-start) | collective-permute-done | bytes 327712 | tf_op jit(solution)/shard_map/while/body/eval_jaxpr/ppermute | solution.py:9
  136.8 4.4 %fusion.104 = f32[5120,256]{1,0:T(8,128)} fusion(f32[5120,256]{1,0:T(8,128)} %get-tuple-element.280, s32[]{:T(128)S(6)} %select_n.39, f32[640,256]{1,0:T(8,128)S(1)} %fusion.103, f32[256,512]{1,0:T(8,128)S(1)} %get-tuple-element.300, f32[5120,512]{0,1:T(8,128)} %get-tuple-element.299), kind=kOutput, calls=%fused_computation.3.clone.1 | convolution fusion | flops 1006796800 | bytes 3146752 | tf_op jit(solution)/shard_map/while/body/eval_jaxpr/dot_general | solution.py:13
  141.3 8.3 %collective-permute-done = f32[640,128]{1,0:T(8,128)S(1)} collective-permute-done((f32[640,128]{1,0:T(8,128)S(1)}, f32[640,128]{1,0:T(8,128)S(1)}, u32[]{:S(2)}, u32[]{:S(2)}) %collective-permute-start) | collective-permute-done | bytes 327712 | tf_op jit(solution)/shard_map/while/body/eval_jaxpr/ppermute | solution.py:9
  150.5 4.4 %fusion.104 = f32[5120,256]{1,0:T(8,128)} fusion(f32[5120,256]{1,0:T(8,128)} %get-tuple-element.280, s32[]{:T(128)S(6)} %select_n.39, f32[640,256]{1,0:T(8,128)S(1)} %fusion.103, f32[256,512]{1,0:T(8,128)S(1)} %get-tuple-element.300, f32[5120,512]{0,1:T(8,128)} %get-tuple-element.299), kind=kOutput, calls=%fused_computation.3.clone.1 | convolution fusion | flops 1006796800 | bytes 3146752 | tf_op jit(solution)/shard_map/while/body/eval_jaxpr/dot_general | solution.py:13
  155.0 8.3 %collective-permute-done = f32[640,128]{1,0:T(8,128)S(1)} collective-permute-done((f32[640,128]{1,0:T(8,128)S(1)}, f32[640,128]{1,0:T(8,128)S(1)}, u32[]{:S(2)}, u32[]{:S(2)}) %collective-permute-start) | collective-permute-done | bytes 327712 | tf_op jit(solution)/shard_map/while/body/eval_jaxpr/ppermute | solution.py:9
  164.1 4.4 %fusion.104 = f32[5120,256]{1,0:T(8,128)} fusion(f32[5120,256]{1,0:T(8,128)} %get-tuple-element.280, s32[]{:T(128)S(6)} %select_n.39, f32[640,256]{1,0:T(8,128)S(1)} %fusion.103, f32[256,512]{1,0:T(8,128)S(1)} %get-tuple-element.300, f32[5120,512]{0,1:T(8,128)} %get-tuple-element.299), kind=kOutput, calls=%fused_computation.3.clone.1 | convolution fusion | flops 1006796800 | bytes 3146752 | tf_op jit(solution)/shard_map/while/body/eval_jaxpr/dot_general | solution.py:13
  168.6 8.3 %collective-permute-done = f32[640,128]{1,0:T(8,128)S(1)} collective-permute-done((f32[640,128]{1,0:T(8,128)S(1)}, f32[640,128]{1,0:T(8,128)S(1)}, u32[]{:S(2)}, u32[]{:S(2)}) %collective-permute-start) | collective-permute-done | bytes 327712 | tf_op jit(solution)/shard_map/while/body/eval_jaxpr/ppermute | solution.py:9
  177.8 4.4 %fusion.104 = f32[5120,256]{1,0:T(8,128)} fusion(f32[5120,256]{1,0:T(8,128)} %get-tuple-element.280, s32[]{:T(128)S(6)} %select_n.39, f32[640,256]{1,0:T(8,128)S(1)} %fusion.103, f32[256,512]{1,0:T(8,128)S(1)} %get-tuple-element.300, f32[5120,512]{0,1:T(8,128)} %get-tuple-element.299), kind=kOutput, calls=%fused_computation.3.clone.1 | convolution fusion | flops 1006796800 | bytes 3146752 | tf_op jit(solution)/shard_map/while/body/eval_jaxpr/dot_general | solution.py:13
  182.3 8.3 %collective-permute-done = f32[640,128]{1,0:T(8,128)S(1)} collective-permute-done((f32[640,128]{1,0:T(8,128)S(1)}, f32[640,128]{1,0:T(8,128)S(1)}, u32[]{:S(2)}, u32[]{:S(2)}) %collective-permute-start) | collective-permute-done | bytes 327712 | tf_op jit(solution)/shard_map/while/body/eval_jaxpr/ppermute | solution.py:9
  191.5 4.4 %fusion.104 = f32[5120,256]{1,0:T(8,128)} fusion(f32[5120,256]{1,0:T(8,128)} %get-tuple-element.280, s32[]{:T(128)S(6)} %select_n.39, f32[640,256]{1,0:T(8,128)S(1)} %fusion.103, f32[256,512]{1,0:T(8,128)S(1)} %get-tuple-element.300, f32[5120,512]{0,1:T(8,128)} %get-tuple-element.299), kind=kOutput, calls=%fused_computation.3.clone.1 | convolution fusion | flops 1006796800 | bytes 3146752 | tf_op jit(solution)/shard_map/while/body/eval_jaxpr/dot_general | solution.py:13
  196.0 8.3 %collective-permute-done = f32[640,128]{1,0:T(8,128)S(1)} collective-permute-done((f32[640,128]{1,0:T(8,128)S(1)}, f32[640,128]{1,0:T(8,128)S(1)}, u32[]{:S(2)}, u32[]{:S(2)}) %collective-permute-start) | collective-permute-done | bytes 327712 | tf_op jit(solution)/shard_map/while/body/eval_jaxpr/ppermute | solution.py:9
  205.2 4.4 %fusion.104 = f32[5120,256]{1,0:T(8,128)} fusion(f32[5120,256]{1,0:T(8,128)} %get-tuple-element.280, s32[]{:T(128)S(6)} %select_n.39, f32[640,256]{1,0:T(8,128)S(1)} %fusion.103, f32[256,512]{1,0:T(8,128)S(1)} %get-tuple-element.300, f32[5120,512]{0,1:T(8,128)} %get-tuple-element.299), kind=kOutput, calls=%fused_computation.3.clone.1 | convolution fusion | flops 1006796800 | bytes 3146752 | tf_op jit(solution)/shard_map/while/body/eval_jaxpr/dot_general | solution.py:13
  209.7 8.3 %collective-permute-done = f32[640,128]{1,0:T(8,128)S(1)} collective-permute-done((f32[640,128]{1,0:T(8,128)S(1)}, f32[640,128]{1,0:T(8,128)S(1)}, u32[]{:S(2)}, u32[]{:S(2)}) %collective-permute-start) | collective-permute-done | bytes 327712 | tf_op jit(solution)/shard_map/while/body/eval_jaxpr/ppermute | solution.py:9
  218.8 4.4 %fusion.104 = f32[5120,256]{1,0:T(8,128)} fusion(f32[5120,256]{1,0:T(8,128)} %get-tuple-element.280, s32[]{:T(128)S(6)} %select_n.39, f32[640,256]{1,0:T(8,128)S(1)} %fusion.103, f32[256,512]{1,0:T(8,128)S(1)} %get-tuple-element.300, f32[5120,512]{0,1:T(8,128)} %get-tuple-element.299), kind=kOutput, calls=%fused_computation.3.clone.1 | convolution fusion | flops 1006796800 | bytes 3146752 | tf_op jit(solution)/shard_map/while/body/eval_jaxpr/dot_general | solution.py:13
  (52 shorter events, 14.3 us)
Async XLA Ops:
  6.5 8.9 %copy-start.3 = (f32[2,256,256]{2,1,0:T(8,128)S(1)}, f32[2,256,256]{2,1,0:T(8,128)}, u32[]{:S(2)}) copy-start(f32[2,256,256]{2,1,0:T(8,128)} %param.9) | copy-start | bytes 1572868
  6.5 114.8 %all-gather.2.cloned.1.call-start = ((), (), s32[]{:S(2)}) async-start(), calls=%async_computation | async-start | bytes 11796480 | tf_op jit(solution)/shard_map/all_gather | solution.py:42
  12.2 6.9 %copy-start = (f32[256,128]{1,0:T(8,128)S(1)}, f32[256,128]{1,0:T(8,128)}, u32[]{:S(2)}) copy-start(f32[256,128]{1,0:T(8,128)} %param.7) | copy-start | bytes 393220
  13.6 5.6 %copy-start.2 = (f32[2,256,128]{2,1,0:T(8,128)S(1)}, f32[2,256,128]{2,1,0:T(8,128)}, u32[]{:S(2)}) copy-start(f32[2,256,128]{2,1,0:T(8,128)} %param.8) | copy-start | bytes 786436
  125.2 2.4 %copy-start.1 = (f32[5120,256]{1,0:T(8,128)}, f32[5120,256]{1,0:T(8,128)S(1)}, u32[]{:S(2)}) copy-start(f32[5120,256]{1,0:T(8,128)S(1)} %fusion.18) | copy-start | bytes 15728644
  127.6 8.3 %collective-permute-start = (f32[640,128]{1,0:T(8,128)S(1)}, f32[640,128]{1,0:T(8,128)S(1)}, u32[]{:S(2)}, u32[]{:S(2)}) collective-permute-start(f32[640,128]{1,0:T(8,128)S(1)} %get-tuple-element.281), channel_id=1, source_target_pairs={{0,1},{1,2},{2,3},{3,4},{4,5},{5,6},{6,7},{7,0},{8,9},{9,10},{10,1... | collective-permute-start | bytes 983048 | tf_op jit(solution)/shard_map/while/body/eval_jaxpr/ppermute | solution.py:9
  141.2 8.3 %collective-permute-start = (f32[640,128]{1,0:T(8,128)S(1)}, f32[640,128]{1,0:T(8,128)S(1)}, u32[]{:S(2)}, u32[]{:S(2)}) collective-permute-start(f32[640,128]{1,0:T(8,128)S(1)} %get-tuple-element.281), channel_id=1, source_target_pairs={{0,1},{1,2},{2,3},{3,4},{4,5},{5,6},{6,7},{7,0},{8,9},{9,10},{10,1... | collective-permute-start | bytes 983048 | tf_op jit(solution)/shard_map/while/body/eval_jaxpr/ppermute | solution.py:9
  154.9 8.3 %collective-permute-start = (f32[640,128]{1,0:T(8,128)S(1)}, f32[640,128]{1,0:T(8,128)S(1)}, u32[]{:S(2)}, u32[]{:S(2)}) collective-permute-start(f32[640,128]{1,0:T(8,128)S(1)} %get-tuple-element.281), channel_id=1, source_target_pairs={{0,1},{1,2},{2,3},{3,4},{4,5},{5,6},{6,7},{7,0},{8,9},{9,10},{10,1... | collective-permute-start | bytes 983048 | tf_op jit(solution)/shard_map/while/body/eval_jaxpr/ppermute | solution.py:9
  168.6 8.3 %collective-permute-start = (f32[640,128]{1,0:T(8,128)S(1)}, f32[640,128]{1,0:T(8,128)S(1)}, u32[]{:S(2)}, u32[]{:S(2)}) collective-permute-start(f32[640,128]{1,0:T(8,128)S(1)} %get-tuple-element.281), channel_id=1, source_target_pairs={{0,1},{1,2},{2,3},{3,4},{4,5},{5,6},{6,7},{7,0},{8,9},{9,10},{10,1... | collective-permute-start | bytes 983048 | tf_op jit(solution)/shard_map/while/body/eval_jaxpr/ppermute | solution.py:9
  182.2 8.3 %collective-permute-start = (f32[640,128]{1,0:T(8,128)S(1)}, f32[640,128]{1,0:T(8,128)S(1)}, u32[]{:S(2)}, u32[]{:S(2)}) collective-permute-start(f32[640,128]{1,0:T(8,128)S(1)} %get-tuple-element.281), channel_id=1, source_target_pairs={{0,1},{1,2},{2,3},{3,4},{4,5},{5,6},{6,7},{7,0},{8,9},{9,10},{10,1... | collective-permute-start | bytes 983048 | tf_op jit(solution)/shard_map/while/body/eval_jaxpr/ppermute | solution.py:9
  195.9 8.3 %collective-permute-start = (f32[640,128]{1,0:T(8,128)S(1)}, f32[640,128]{1,0:T(8,128)S(1)}, u32[]{:S(2)}, u32[]{:S(2)}) collective-permute-start(f32[640,128]{1,0:T(8,128)S(1)} %get-tuple-element.281), channel_id=1, source_target_pairs={{0,1},{1,2},{2,3},{3,4},{4,5},{5,6},{6,7},{7,0},{8,9},{9,10},{10,1... | collective-permute-start | bytes 983048 | tf_op jit(solution)/shard_map/while/body/eval_jaxpr/ppermute | solution.py:9
  209.6 8.3 %collective-permute-start = (f32[640,128]{1,0:T(8,128)S(1)}, f32[640,128]{1,0:T(8,128)S(1)}, u32[]{:S(2)}, u32[]{:S(2)}) collective-permute-start(f32[640,128]{1,0:T(8,128)S(1)} %get-tuple-element.281), channel_id=1, source_target_pairs={{0,1},{1,2},{2,3},{3,4},{4,5},{5,6},{6,7},{7,0},{8,9},{9,10},{10,1... | collective-permute-start | bytes 983048 | tf_op jit(solution)/shard_map/while/body/eval_jaxpr/ppermute | solution.py:9
Sparse Core Ops, SparseCore 0:
  19.2 102.0 all-gather.1
where the time goes:
time: 231 us; the launch traced here: 230 us
  waiting for transfers between devices  156 us (68%)
  matrix products  51.2 us (22%)
  between operations  13.6 us (6%)
  local copies, waits for them, and re-layouts  4.09 us (2%)
  other arithmetic  3.79 us (2%)
    all_gather x1, waiting for transfers between devices, local(): lax.all_gather(factors(landmarks, panel_points, inverse_blocks, first_nex...  98.9 us
    ppermute x7, waiting for transfers between devices, passed_along(): lax.ppermute(shard, axis, [(i, (i + by) % size) for i in range(size)])  57.6 us
    dot_general x28, matrix products, dot_rows(): lax.dot_general(left_matrix, right_matrix, (((1,), (1,)), ((), ())), prec...  51.2 us
  transfers between devices with their start and end apart: 8, of which 8 were waited for; matrix products, arithmetic and copies ran while one was open for 1% of the time, Pallas kernels for 0%

commit v1 on v0

v1 whole, which is shorter than its diff:
```python
import functools
import math

import jax
import jax.numpy as jnp
from jax import lax
from jax.experimental import pallas as pl
from jax.experimental.pallas import tpu as pltpu
from jax.sharding import PartitionSpec as P

LOG2E = math.log2(math.e)
CHUNK = 160


def dot(left, right, left_dim=1, right_dim=0, precision=None):
    return lax.dot_general(
        left,
        right,
        (((left_dim,), (right_dim,)), ((), ())),
        precision=precision,
        preferred_element_type=jnp.float32,
    )


exact_dot = functools.partial(dot, precision=lax.Precision.HIGHEST)


def split(value):
    high = value.astype(jnp.bfloat16)
    low = (value - high.astype(jnp.float32)).astype(jnp.bfloat16)
    return high, low


def norm_lanes(norm, index, at):
    first = norm.astype(jnp.bfloat16).astype(jnp.float32)
    second = (norm - first).astype(jnp.bfloat16).astype(jnp.float32)
    third = norm - first - second
    lanes = jnp.where(index < 6, 1.0, 0.0)
    lanes = jnp.where(index == at, first, lanes)
    lanes = jnp.where(index == at + 1, second, lanes)
    return jnp.where(index == at + 2, third, lanes).astype(jnp.bfloat16)


def setup_kernel(slab_hbm, panel_hbm, inverse_hbm, points_ref, weights_ref, slab_ref, panel_ref, inverse_ref, sems):
    dim, panel = slab_ref.shape[1], panel_ref.shape[1]
    pairs = ((panel_hbm, panel_ref), (slab_hbm, slab_ref), (inverse_hbm, inverse_ref))
    copies = [pltpu.make_async_copy(source, held, sems.at[i]) for i, (source, held) in enumerate(pairs)]
    for copy in copies:
        copy.start()
    for copy in copies:
        copy.wait()
    panels = [panel_ref[0], panel_ref[1]]
    inverse = [inverse_ref[0], inverse_ref[1]]
    columns = jnp.concatenate([*panels, slab_ref[...]], axis=0).T
    norms = jnp.sum(columns * columns, axis=0, keepdims=True)

    high, low = split(columns * (2.0 * LOG2E / dim))
    index = lax.broadcasted_iota(jnp.int32, columns.shape, 0)
    lanes = norm_lanes(norms * (-LOG2E / dim), index, 3)
    points_ref[...] = jnp.concatenate([high, low, high, lanes], axis=0)

    def gaussian(rows, start):
        row_norms = jnp.sum(rows * rows, axis=1, keepdims=True)
        inner = exact_dot(rows, columns[:, start:])
        return jnp.exp((2.0 * inner - row_norms - norms[:, start:]) / dim)

    firsts = exact_dot(inverse[0], gaussian(panels[0], panel))
    first_next, slab_first = firsts[:, :panel], firsts[:, panel:]
    raw = gaussian(panels[1], 2 * panel) - exact_dot(first_next, slab_first, 0, 0)
    slab_second = exact_dot(inverse[1], raw)
    second = exact_dot(inverse[1], slab_second, 0, 0)
    first = exact_dot(inverse[0], slab_first - exact_dot(first_next, second), 0, 0)
    high, low = split(jnp.concatenate([first, second], axis=0))
    weights_ref[...] = jnp.concatenate([high, low, high], axis=0)


def setup(slab_points, panel_points, inverse_blocks):
    columns, dim = slab_points.shape
    panel = panel_points.shape[1]
    vmem = pl.BlockSpec(memory_space=pltpu.VMEM)
    operands = (slab_points, panel_points, inverse_blocks)
    return pl.pallas_call(
        setup_kernel,
        out_shape=(
            jax.ShapeDtypeStruct((4 * dim, 2 * panel + columns), jnp.bfloat16),
            jax.ShapeDtypeStruct((6 * panel, columns), jnp.bfloat16),
        ),
        in_specs=[pl.BlockSpec(memory_space=pltpu.HBM)] * 3,
        out_specs=(vmem, vmem),
        scratch_shapes=[pltpu.VMEM(x.shape, x.dtype) for x in operands] + [pltpu.SemaphoreType.DMA((3,))],
        compiler_params=pltpu.CompilerParams(vmem_limit_bytes=32 << 20),
        cost_estimate=pl.CostEstimate(
            flops=100 * panel**3, bytes_accessed=4 << 20, transcendentals=3 * panel * panel
        ),
        name="setup",
    )(*operands)


def block_result(points, column_points, weights):
    dim = points.shape[1]
    panels = weights.shape[0] // 3
    high, low = split(points)
    norm = jnp.sum(points * points, axis=1, keepdims=True) * (-LOG2E / dim)
    lanes = norm_lanes(norm, lax.broadcasted_iota(jnp.int32, points.shape, 1), 0)
    kernel = jnp.exp2(dot(jnp.concatenate([high, high, low, lanes], axis=1), column_points))
    high, low = split(kernel[:, :panels])
    return kernel[:, panels:] - dot(jnp.concatenate([high, high, low], axis=1), weights)


def update_kernel(places, block_rows, *refs):
    blocks, (points_ref, weights_ref) = refs[: len(places)], refs[len(places) : len(places) + 2]
    out_ref, held, sems = refs[-3:]
    me = lax.axis_index("col")
    copies, done = [], 0
    for (mask, first_row), block in zip(places, blocks):
        for at in range(0, block.shape[0], CHUNK):
            size = min(CHUNK, block.shape[0] - at)
            held[done : done + size, :] = block_result(
                block[at : at + size, :], points_ref[...], weights_ref[...]
            )
            row = pl.multiple_of(jnp.bitwise_xor(me, mask) * block_rows + first_row + at, 8)
            copy = pltpu.make_async_copy(
                held.at[pl.ds(done, size), :], out_ref.at[pl.ds(row, size), :], sems.at[len(copies)]
            )
            copy.start()
            copies.append(copy)
            done += size
    for copy in copies:
        copy.wait()


def update(out, block_rows, pieces, column_points, weights):
    places = [(mask, first_row) for mask, first_row, _ in pieces]
    blocks = [block for _, _, block in pieces]
    rows = sum(block.shape[0] for block in blocks)
    chunks = sum(-(-block.shape[0] // CHUNK) for block in blocks)
    columns = weights.shape[1]
    vmem = pl.BlockSpec(memory_space=pltpu.VMEM)
    hbm = pl.BlockSpec(memory_space=pltpu.HBM)
    operands = [*blocks, column_points, weights]
    in_specs = [vmem] * (len(blocks) + 2)
    aliases = {}
    if out is not None:
        aliases = {len(operands): 0}
        operands.append(out)
        in_specs.append(hbm)
    return pl.pallas_call(
        functools.partial(update_kernel, places, block_rows),
        out_shape=jax.ShapeDtypeStruct((block_rows * lax.axis_size("col"), columns), jnp.float32),
        in_specs=in_specs,
        out_specs=hbm,
        scratch_shapes=[pltpu.VMEM((rows, columns), jnp.float32), pltpu.SemaphoreType.DMA((chunks,))],
        input_output_aliases=aliases,
        compiler_params=pltpu.CompilerParams(vmem_limit_bytes=32 << 20),
        cost_estimate=pl.CostEstimate(flops=10**10, bytes_accessed=0, transcendentals=0),
        name="update",
    )(*operands)


def swapped(pieces, mask):
    pairs = [(i, i ^ mask) for i in range(lax.axis_size("col"))]
    return [(held ^ mask, row, lax.ppermute(block, "col", pairs)) for held, row, block in pieces]


def cut(pieces, row):
    first = [(mask, at, block[:row]) for mask, at, block in pieces]
    return first, [(mask, at + row, block[row:]) for mask, at, block in pieces]


def after(out, pieces):
    out, *blocks = lax.optimization_barrier((out, *[block for _, _, block in pieces]))
    return out, [(mask, row, block) for (mask, row, _), block in zip(pieces, blocks)]


def local(landmarks, slab_points, panel_points, inverse_blocks):
    size = lax.axis_size("col")
    rows = landmarks.shape[0]
    own = [(0, 0, landmarks)]
    bits = [1 << i for i in reversed(range(1, size.bit_length() - 1))]
    direct = [swapped(own, bit) for bit in bits]
    near = swapped(own, 1)
    column_points, weights = setup(slab_points, panel_points, inverse_blocks)

    def computed(out, pieces):
        return update(out, rows, pieces, column_points, weights)

    out = computed(None, own + near)
    fresh, held = direct[0], []
    for bit, came in zip(bits[1:], direct[1:]):
        out, fresh = after(out, fresh)
        held = held + fresh
        if bit > 2:
            moved = [swapped(held, bit)]
        else:
            moved = [swapped(part, bit) for part in cut(held, rows // 16 * 8)]
        near = swapped(fresh, 1)
        out, came = after(out, came)
        out = computed(out, fresh + near + came + swapped(came, 1))
        held = held + came
        fresh = moved[0]
    out, first = after(out, moved[0])
    near = swapped(first, 1)
    out, second = after(out, moved[1])
    far = swapped(second, 1)
    out = computed(out, first + near + second)
    return computed(out, far)


def solution(mesh):
    in_specs = (P(("row", "col"), None), P("col", None), P(), P())
    out_specs = P("row", "col")
    return jax.shard_map(local, mesh=mesh, in_specs=in_specs, out_specs=out_specs, check_vma=False)
```

time: 231 us -> 34.7 us (0.15)
  waiting for transfers between devices: 156 us -> 6.19 us
  matrix products: 51.2 us -> 0 us
  Pallas kernels: 0 us -> 16.9 us
  between operations: 13.6 us -> 0.09 us
  starting transfers between devices: 0.6 us -> 8.29 us
  other arithmetic: 3.79 us -> 0 us
    all_gather x1 -> x0, waiting for transfers between devices: 98.9 us -> none  [local(): lax.all_gather(factors(landmarks, panel_points, inverse_blocks, first_nex...]
    ppermute x7 -> x9, waiting for transfers between devices: 57.6 us -> 6.19 us  [swapped(): lax.ppermute(block, 'col', pairs)]
    dot_general x28 -> x0, matrix products: 51.2 us -> none  [dot_rows(): lax.dot_general(left_matrix, right_matrix, (((1,), (1,)), ((), ())), prec...]
    pallas_call x0 -> x5, Pallas kernels: none -> 16.9 us  [the longest x4 12.7 us: update(): pl.pallas_call(functools.partial(update_kernel, places, block_rows), out_...]
    ppermute x7 -> x9, starting transfers between devices: 0.6 us -> 8.29 us  [swapped(): lax.ppermute(block, 'col', pairs)]
    reduce_sum x10 -> x0, other arithmetic: 2.61 us -> none  [the longest x8 1.38 us: gaussian(): left_norms = jnp.sum(left_points * left_points, axis=1)[:, None]]
  transfers between devices with their start and end apart: 8 -> 9, of which waited for: 8 -> 3; matrix products, arithmetic and copies ran while one was open for 1% -> 0% of each run, Pallas kernels for 0% -> 45%
where the time goes in v1:
time: 34.7 us; the launch traced here: 34.4 us
  Pallas kernels  16.9 us (49%)
  starting transfers between devices  8.29 us (24%)
  waiting for transfers between devices  6.19 us (18%)
  local copies, waits for them, and re-layouts  2.92 us (8%)
    pallas_call x4, Pallas kernels, update(): pl.pallas_call(functools.partial(update_kernel, places, block_rows), out_...  12.7 us
    ppermute x9, starting transfers between devices, swapped(): lax.ppermute(block, 'col', pairs)  8.29 us
    ppermute x9, waiting for transfers between devices, swapped(): lax.ppermute(block, 'col', pairs)  6.19 us
    pallas_call x1, Pallas kernels, setup(): pl.pallas_call(setup_kernel, out_shape=(jax.ShapeDtypeStruct((4 * dim, 2...  4.23 us
    unnamed x8, local copies, waits for them, and re-layouts  2.9 us
  transfers between devices with their start and end apart: 9, of which 3 were waited for; matrix products, arithmetic and copies ran while one was open for 0% of the time, Pallas kernels for 45%

profile of v1, /device:TPU:0, one launch (start us, length us, event | category | flops | bytes accessed | tf_op | source)
XLA Modules:
  0.0 34.4 jit_solution(7460535225343846751)
XLA Ops:
  0.0 0.5 %collective-permute-start = (f32[640,128]{1,0:T(8,128)}, f32[640,128]{1,0:T(8,128)S(1)}, u32[]{:S(2)}, u32[]{:S(2)}) collective-permute-start(f32[640,128]{1,0:T(8,128)} %refs_0_.1), channel_id=1, source_target_pairs={{0,1},{1,0},{2,3},{3,2},{4,5},{5,4},{6,7},{7,6},{8,9},{9,8},{10,11... | collective-permute-start | bytes 983048 | tf_op jit(solution)/shard_map/ppermute | solution.py:162
  0.5 3.6 %collective-permute-start.1 = (f32[640,128]{1,0:T(8,128)}, f32[640,128]{1,0:T(8,128)S(1)}, u32[]{:S(2)}, u32[]{:S(2)}) collective-permute-start(f32[640,128]{1,0:T(8,128)} %refs_0_.1), channel_id=1, source_target_pairs={{0,4},{1,5},{2,6},{3,7},{4,0},{5,1},{6,2},{7,3},{8,12},{9,13},{10,... | collective-permute-start | bytes 983048 | tf_op jit(solution)/shard_map/ppermute | solution.py:162
  4.0 1.6 %collective-permute-start.3 = (f32[640,128]{1,0:T(8,128)}, f32[640,128]{1,0:T(8,128)S(1)}, u32[]{:S(2)}, u32[]{:S(2)}) collective-permute-start(f32[640,128]{1,0:T(8,128)} %refs_0_.1), channel_id=1, source_target_pairs={{0,2},{1,3},{2,0},{3,1},{4,6},{5,7},{6,4},{7,5},{8,10},{9,11},{10,... | collective-permute-start | bytes 983048 | tf_op jit(solution)/shard_map/ppermute | solution.py:162
  5.6 1.0 %copy-done = f32[2,256,256]{2,1,0:T(8,128)S(1)} copy-done((f32[2,256,256]{2,1,0:T(8,128)S(1)}, f32[2,256,256]{2,1,0:T(8,128)}, u32[]{:S(2)}) %copy-start) | copy-done | bytes 524312
  6.7 0.9 %copy-done.2 = f32[2,256,128]{2,1,0:T(8,128)S(1)} copy-done((f32[2,256,128]{2,1,0:T(8,128)S(1)}, f32[2,256,128]{2,1,0:T(8,128)}, u32[]{:S(2)}) %copy-start.2) | copy-done | bytes 262168
  7.6 0.9 %copy-done.3 = f32[256,128]{1,0:T(8,128)S(1)} copy-done((f32[256,128]{1,0:T(8,128)S(1)}, f32[256,128]{1,0:T(8,128)}, u32[]{:S(2)}) %copy-start.3) | copy-done | bytes 131096
  8.5 4.2 %setup.1 = (bf16[512,768]{1,0:T(8,128)(2,1)S(1)}, bf16[1536,256]{1,0:T(8,128)(2,1)S(1)}) custom-call(f32[256,128]{1,0:T(8,128)S(1)} %copy-done.3, f32[2,256,128]{2,1,0:T(8,128)S(1)} %copy-done.2, f32[2,256,256]{2,1,0:T(8,128)S(1)} %copy-done), custom_call_target="tpu_custom_call" | custom-call | flops 1677721600 | bytes 4194304 | tf_op jit(solution)/shard_map/setup/pallas_call | solution.py:82
  12.8 0.0 collective-permute-done.refs_1_
  12.8 3.2 %update.4.refs_6_ = f32[5120,256]{1,0:T(8,128)} custom-call(f32[640,128]{1,0:T(8,128)S(1)} %copy-done.1, f32[640,128]{1,0:T(8,128)S(1)} %collective-permute-done.refs_1_, bf16[512,768]{1,0:T(8,128)(2,1)S(1)} %get-tuple-element.15.refs_2_.refs_4_.refs_3_.refs_1_, bf16[1536,256]{1,0:T(8,128)(2,1)S(1)} %get-tuple-element.16.refs_3_.refs_5_.refs_4_.refs_2_), custom_call_target="tpu_custom_call" | custom-call | flops 10000000000 | tf_op jit(solution)/shard_map/update/pallas_call | solution.py:147
  16.0 3.8 %collective-permute-done.1.refs_0_ = f32[640,128]{1,0:T(8,128)S(1)} collective-permute-done((f32[640,128]{1,0:T(8,128)}, f32[640,128]{1,0:T(8,128)S(1)}, u32[]{:S(2)}, u32[]{:S(2)}) %collective-permute-start.1) | collective-permute-done | bytes 327712 | tf_op jit(solution)/shard_map/ppermute | solution.py:162
  19.8 0.2 collective-permute-done.3.refs_2_
  19.9 0.0 collective-permute-start.4
  20.0 0.5 %collective-permute-start.2 = (f32[640,128]{1,0:T(8,128)S(1)}, f32[640,128]{1,0:T(8,128)S(1)}, u32[]{:S(2)}, u32[]{:S(2)}) collective-permute-start(f32[640,128]{1,0:T(8,128)S(1)} %collective-permute-done.1.refs_0_), channel_id=1, source_target_pairs={{0,1},{1,0},{2,3},{3,2},{4,5},{5,4},{6,7},{7,6},{8,9},{9,8},{10,11... | collective-permute-start | bytes 983048 | tf_op jit(solution)/shard_map/ppermute | solution.py:162
  20.5 1.6 %collective-permute-start.5 = (f32[320,128]{1,0:T(8,128)S(1)}, f32[320,128]{1,0:T(8,128)S(1)}, u32[]{:S(2)}, u32[]{:S(2)}) collective-permute-start(f32[320,128]{1,0:T(8,128)S(1)} %get-tuple-element.26), channel_id=1, source_target_pairs={{0,2},{1,3},{2,0},{3,1},{4,6},{5,7},{6,4},{7,5},{8,10},{9,11},{10,... | collective-permute-start | bytes 491528 | tf_op jit(solution)/shard_map/ppermute | solution.py:162
  22.0 0.5 %collective-permute-start.6 = (f32[320,128]{1,0:T(8,128)S(1)}, f32[320,128]{1,0:T(8,128)S(1)}, u32[]{:S(2)}, u32[]{:S(2)}) collective-permute-start(f32[320,128]{1,0:T(8,128)S(1)} %get-tuple-element.25), channel_id=1, source_target_pairs={{0,2},{1,3},{2,0},{3,1},{4,6},{5,7},{6,4},{7,5},{8,10},{9,11},{10,... | collective-permute-start | bytes 491528 | tf_op jit(solution)/shard_map/ppermute | solution.py:162
  22.6 0.0 collective-permute-done.2.refs_1_
  22.6 5.3 %update.5.refs_5_ = f32[5120,256]{1,0:T(8,128)} custom-call(f32[640,128]{1,0:T(8,128)S(1)} %collective-permute-done.1.refs_0_, f32[640,128]{1,0:T(8,128)S(1)} %collective-permute-done.2.refs_1_, f32[640,128]{1,0:T(8,128)S(1)} %collective-permute-done.3.refs_2_, f32[640,128]{1,0:T(8,128)S(1)} %collective-permute-done.4.refs_3_, ...), custom_call_target="tpu_custom_call", output_to_operand_aliasing={{}: (6, {})} | custom-call | flops 10000000000 | tf_op jit(solution)/shard_map/update/pallas_call | solution.py:147
  27.9 0.1 collective-permute-start.8
  28.0 2.2 %collective-permute-done.6.refs_2_ = f32[320,128]{1,0:T(8,128)S(1)} collective-permute-done((f32[320,128]{1,0:T(8,128)S(1)}, f32[320,128]{1,0:T(8,128)S(1)}, u32[]{:S(2)}, u32[]{:S(2)}) %collective-permute-start.6) | collective-permute-done | bytes 163872 | tf_op jit(solution)/shard_map/ppermute | solution.py:162
  30.2 0.0 collective-permute-start.7
  30.2 0.0 collective-permute-done.8.refs_1_
  30.2 2.6 %update.6.refs_3_ = f32[5120,256]{1,0:T(8,128)} custom-call(f32[320,128]{1,0:T(8,128)S(1)} %collective-permute-done.5.refs_0_, f32[320,128]{1,0:T(8,128)S(1)} %collective-permute-done.8.refs_1_, f32[320,128]{1,0:T(8,128)S(1)} %collective-permute-done.6.refs_2_, ...), custom_call_target="tpu_custom_call", output_to_operand_aliasing={{}: (5, {})} | custom-call | flops 10000000000 | tf_op jit(solution)/shard_map/update/pallas_call | solution.py:147
  32.8 0.0 collective-permute-done.7.refs_0_
  32.8 1.6 %update.7 = f32[5120,256]{1,0:T(8,128)} custom-call(f32[320,128]{1,0:T(8,128)S(1)} %collective-permute-done.7.refs_0_, bf16[512,768]{1,0:T(8,128)(2,1)S(1)} %get-tuple-element.15.refs_2_.refs_4_.refs_3_.refs_1_, bf16[1536,256]{1,0:T(8,128)(2,1)S(1)} %get-tuple-element.16.refs_3_.refs_5_.refs_4_.refs_2_, ...), custom_call_target="tpu_custom_call", output_to_operand_aliasing={{}: (3, {})} | custom-call | flops 10000000000 | tf_op jit(solution)/shard_map/update/pallas_call | solution.py:147
  (8 shorter events, 0.0 us)
Async XLA Ops:
  0.0 12.8 %collective-permute-start = (f32[640,128]{1,0:T(8,128)}, f32[640,128]{1,0:T(8,128)S(1)}, u32[]{:S(2)}, u32[]{:S(2)}) collective-permute-start(f32[640,128]{1,0:T(8,128)} %refs_0_.1), channel_id=1, source_target_pairs={{0,1},{1,0},{2,3},{3,2},{4,5},{5,4},{6,7},{7,6},{8,9},{9,8},{10,11... | collective-permute-start | bytes 983048 | tf_op jit(solution)/shard_map/ppermute | solution.py:162
  0.5 19.3 %collective-permute-start.1 = (f32[640,128]{1,0:T(8,128)}, f32[640,128]{1,0:T(8,128)S(1)}, u32[]{:S(2)}, u32[]{:S(2)}) collective-permute-start(f32[640,128]{1,0:T(8,128)} %refs_0_.1), channel_id=1, source_target_pairs={{0,4},{1,5},{2,6},{3,7},{4,0},{5,1},{6,2},{7,3},{8,12},{9,13},{10,... | collective-permute-start | bytes 983048 | tf_op jit(solution)/shard_map/ppermute | solution.py:162
  4.0 15.9 %collective-permute-start.3 = (f32[640,128]{1,0:T(8,128)}, f32[640,128]{1,0:T(8,128)S(1)}, u32[]{:S(2)}, u32[]{:S(2)}) collective-permute-start(f32[640,128]{1,0:T(8,128)} %refs_0_.1), channel_id=1, source_target_pairs={{0,2},{1,3},{2,0},{3,1},{4,6},{5,7},{6,4},{7,5},{8,10},{9,11},{10,... | collective-permute-start | bytes 983048 | tf_op jit(solution)/shard_map/ppermute | solution.py:162
  5.6 1.0 %copy-start = (f32[2,256,256]{2,1,0:T(8,128)S(1)}, f32[2,256,256]{2,1,0:T(8,128)}, u32[]{:S(2)}) copy-start(f32[2,256,256]{2,1,0:T(8,128)} %inverse_hbm.1) | copy-start | bytes 1572868
  6.7 0.9 %copy-start.2 = (f32[2,256,128]{2,1,0:T(8,128)S(1)}, f32[2,256,128]{2,1,0:T(8,128)}, u32[]{:S(2)}) copy-start(f32[2,256,128]{2,1,0:T(8,128)} %panel_hbm.1) | copy-start | bytes 786436
  7.6 0.9 %copy-start.3 = (f32[256,128]{1,0:T(8,128)S(1)}, f32[256,128]{1,0:T(8,128)}, u32[]{:S(2)}) copy-start(f32[256,128]{1,0:T(8,128)} %slab_hbm.1) | copy-start | bytes 393220
  8.5 4.2 %copy-start.1 = (f32[640,128]{1,0:T(8,128)S(1)}, f32[640,128]{1,0:T(8,128)}, u32[]{:S(2)}) copy-start(f32[640,128]{1,0:T(8,128)} %refs_0_.1) | copy-start | bytes 983044
  19.9 2.6 %collective-permute-start.4 = (f32[640,128]{1,0:T(8,128)S(1)}, f32[640,128]{1,0:T(8,128)S(1)}, u32[]{:S(2)}, u32[]{:S(2)}) collective-permute-start(f32[640,128]{1,0:T(8,128)S(1)} %collective-permute-done.3.refs_2_), channel_id=1, source_target_pairs={{0,1},{1,0},{2,3},{3,2},{4,5},{5,4},{6,7},{7,6},{8,9},{9,8},{10,11... | collective-permute-start | bytes 983048 | tf_op jit(solution)/shard_map/ppermute | solution.py:162
  20.0 2.6 %collective-permute-start.2 = (f32[640,128]{1,0:T(8,128)S(1)}, f32[640,128]{1,0:T(8,128)S(1)}, u32[]{:S(2)}, u32[]{:S(2)}) collective-permute-start(f32[640,128]{1,0:T(8,128)S(1)} %collective-permute-done.1.refs_0_), channel_id=1, source_target_pairs={{0,1},{1,0},{2,3},{3,2},{4,5},{5,4},{6,7},{7,6},{8,9},{9,8},{10,11... | collective-permute-start | bytes 983048 | tf_op jit(solution)/shard_map/ppermute | solution.py:162
  20.5 7.4 %collective-permute-start.5 = (f32[320,128]{1,0:T(8,128)S(1)}, f32[320,128]{1,0:T(8,128)S(1)}, u32[]{:S(2)}, u32[]{:S(2)}) collective-permute-start(f32[320,128]{1,0:T(8,128)S(1)} %get-tuple-element.26), channel_id=1, source_target_pairs={{0,2},{1,3},{2,0},{3,1},{4,6},{5,7},{6,4},{7,5},{8,10},{9,11},{10,... | collective-permute-start | bytes 491528 | tf_op jit(solution)/shard_map/ppermute | solution.py:162
  22.0 8.1 %collective-permute-start.6 = (f32[320,128]{1,0:T(8,128)S(1)}, f32[320,128]{1,0:T(8,128)S(1)}, u32[]{:S(2)}, u32[]{:S(2)}) collective-permute-start(f32[320,128]{1,0:T(8,128)S(1)} %get-tuple-element.25), channel_id=1, source_target_pairs={{0,2},{1,3},{2,0},{3,1},{4,6},{5,7},{6,4},{7,5},{8,10},{9,11},{10,... | collective-permute-start | bytes 491528 | tf_op jit(solution)/shard_map/ppermute | solution.py:162
  27.9 2.3 %collective-permute-start.8 = (f32[320,128]{1,0:T(8,128)S(1)}, f32[320,128]{1,0:T(8,128)S(1)}, u32[]{:S(2)}, u32[]{:S(2)}) collective-permute-start(f32[320,128]{1,0:T(8,128)S(1)} %collective-permute-done.5.refs_0_), channel_id=1, source_target_pairs={{0,1},{1,0},{2,3},{3,2},{4,5},{5,4},{6,7},{7,6},{8,9},{9,8},{10,11... | collective-permute-start | bytes 491528 | tf_op jit(solution)/shard_map/ppermute | solution.py:162
  30.2 2.7 %collective-permute-start.7 = (f32[320,128]{1,0:T(8,128)S(1)}, f32[320,128]{1,0:T(8,128)S(1)}, u32[]{:S(2)}, u32[]{:S(2)}) collective-permute-start(f32[320,128]{1,0:T(8,128)S(1)} %collective-permute-done.6.refs_2_), channel_id=1, source_target_pairs={{0,1},{1,0},{2,3},{3,2},{4,5},{5,4},{6,7},{7,6},{8,9},{9,8},{10,11... | collective-permute-start | bytes 491528 | tf_op jit(solution)/shard_map/ppermute | solution.py:162

commit v2 on v1

v2 whole, which is shorter than its diff:
```python
import functools
import math

import jax
import jax.numpy as jnp
from jax import lax
from jax.experimental import pallas as pl
from jax.experimental.pallas import tpu as pltpu
from jax.sharding import PartitionSpec as P

LOG2E = math.log2(math.e)
CHUNK = 160
VMEM_BYTES = 16 << 20
SETUP_FLOPS = 17 * 10**8
UPDATE_FLOPS = 10**9
UPDATE_BYTES = 10**7
FENCE_FLOPS = 10**10


def dot(left, right, left_dim=1, right_dim=0, precision=None):
    return lax.dot_general(
        left,
        right,
        (((left_dim,), (right_dim,)), ((), ())),
        precision=precision,
        preferred_element_type=jnp.float32,
    )


exact_dot = functools.partial(dot, precision=lax.Precision.HIGHEST)


def split(value):
    high = value.astype(jnp.bfloat16)
    low = (value - high.astype(jnp.float32)).astype(jnp.bfloat16)
    return high, low


def norm_lanes(norm, index, at):
    first = norm.astype(jnp.bfloat16).astype(jnp.float32)
    second = (norm - first).astype(jnp.bfloat16).astype(jnp.float32)
    third = norm - first - second
    lanes = jnp.where(index < 6, 1.0, 0.0)
    lanes = jnp.where(index == at, first, lanes)
    lanes = jnp.where(index == at + 1, second, lanes)
    return jnp.where(index == at + 2, third, lanes).astype(jnp.bfloat16)


def setup_kernel(slab_hbm, panel_hbm, inverse_hbm, points_ref, weights_ref, out_ref, slab_ref, panel_ref, inverse_ref, sems):
    dim, panel = slab_ref.shape[1], panel_ref.shape[1]
    pairs = ((panel_hbm, panel_ref), (slab_hbm, slab_ref), (inverse_hbm, inverse_ref))
    copies = [pltpu.make_async_copy(source, held, sems.at[i]) for i, (source, held) in enumerate(pairs)]
    for copy in copies:
        copy.start()
    for copy in copies:
        copy.wait()
    panels = [panel_ref[0], panel_ref[1]]
    inverse = [inverse_ref[0], inverse_ref[1]]
    columns = jnp.concatenate([*panels, slab_ref[...]], axis=0).T
    norms = jnp.sum(columns * columns, axis=0, keepdims=True)

    high, low = split(columns * (2.0 * LOG2E / dim))
    index = lax.broadcasted_iota(jnp.int32, columns.shape, 0)
    lanes = norm_lanes(norms * (-LOG2E / dim), index, 3)
    points_ref[...] = jnp.concatenate([high, low, high, lanes], axis=0)

    def gaussian(rows, start):
        row_norms = jnp.sum(rows * rows, axis=1, keepdims=True)
        inner = exact_dot(rows, columns[:, start:])
        return jnp.exp((2.0 * inner - row_norms - norms[:, start:]) / dim)

    firsts = exact_dot(inverse[0], gaussian(panels[0], panel))
    first_next, slab_first = firsts[:, :panel], firsts[:, panel:]
    raw = gaussian(panels[1], 2 * panel) - exact_dot(first_next, slab_first, 0, 0)
    slab_second = exact_dot(inverse[1], raw)
    second = exact_dot(inverse[1], slab_second, 0, 0)
    first = exact_dot(inverse[0], slab_first - exact_dot(first_next, second), 0, 0)
    high, low = split(jnp.concatenate([first, second], axis=0))
    weights_ref[...] = jnp.concatenate([high, low, high], axis=0)


def setup(slab_points, panel_points, inverse_blocks, out_rows):
    columns, dim = slab_points.shape
    panel = panel_points.shape[1]
    vmem = pl.BlockSpec(memory_space=pltpu.VMEM)
    operands = (slab_points, panel_points, inverse_blocks)
    return pl.pallas_call(
        setup_kernel,
        out_shape=(
            jax.ShapeDtypeStruct((4 * dim, 2 * panel + columns), jnp.bfloat16),
            jax.ShapeDtypeStruct((6 * panel, columns), jnp.bfloat16),
            jax.ShapeDtypeStruct((out_rows, columns), jnp.float32),
        ),
        in_specs=[pl.BlockSpec(memory_space=pltpu.HBM)] * 3,
        out_specs=(vmem, vmem, pl.BlockSpec(memory_space=pltpu.HBM)),
        scratch_shapes=[pltpu.VMEM(x.shape, x.dtype) for x in operands] + [pltpu.SemaphoreType.DMA((3,))],
        compiler_params=pltpu.CompilerParams(vmem_limit_bytes=VMEM_BYTES),
        cost_estimate=pl.CostEstimate(
            flops=SETUP_FLOPS, bytes_accessed=4 << 20, transcendentals=3 * panel * panel
        ),
        name="setup",
    )(*operands)


def block_result(points, column_points, weights):
    dim = points.shape[1]
    panels = weights.shape[0] // 3
    high, low = split(points)
    norm = jnp.sum(points * points, axis=1, keepdims=True) * (-LOG2E / dim)
    lanes = norm_lanes(norm, lax.broadcasted_iota(jnp.int32, points.shape, 1), 0)
    kernel = jnp.exp2(dot(jnp.concatenate([high, high, low, lanes], axis=1), column_points))
    high, low = split(kernel[:, :panels])
    return kernel[:, panels:] - dot(jnp.concatenate([high, high, low], axis=1), weights)


def chunks_of(places):
    done, chunks = 0, []
    for mask, first_row, rows in places:
        for at in range(0, rows, CHUNK):
            size = min(CHUNK, rows - at)
            chunks.append((done, mask, first_row + at, size))
            done += size
    return chunks


def update_kernel(places, before, last, block_rows, *refs):
    index_ref, refs = refs[0], refs[1:]
    blocks, (points_ref, weights_ref) = refs[: len(places)], refs[len(places) : len(places) + 2]
    me = index_ref[0]
    out_ref, tile_ref, sems = refs[-3:]
    held_ref = refs[len(places) + 2] if before else None
    copies = []

    def send(source, chunk):
        first, mask, row, size = chunk
        row = pl.multiple_of(jnp.bitwise_xor(me, mask) * block_rows + row, 8)
        copy = pltpu.make_async_copy(
            source.at[pl.ds(first, size), :], out_ref.at[pl.ds(row, size), :], sems.at[len(copies)]
        )
        copy.start()
        copies.append(copy)

    done = 0
    if before:
        for mask, first_row, size in before:
            send(held_ref, (done, mask, first_row, size))
            done += size
    chunks = chunks_of(places)
    piece, used = 0, 0
    for chunk in chunks:
        first, _, _, size = chunk
        if used == places[piece][2]:
            piece, used = piece + 1, 0
        tile_ref[first : first + size, :] = block_result(
            blocks[piece][used : used + size, :], points_ref[...], weights_ref[...]
        )
        used += size
        if last:
            send(tile_ref, chunk)
    for copy in copies:
        copy.wait()


def update(state, index, block_rows, pieces, column_points, weights, last=False):
    out, tile, before = state
    places = [(mask, first_row, block.shape[0]) for mask, first_row, block in pieces]
    rows = sum(place[2] for place in places)
    columns = weights.shape[1]
    vmem = pl.BlockSpec(memory_space=pltpu.VMEM)
    hbm = pl.BlockSpec(memory_space=pltpu.HBM)
    operands = [index] + [block for _, _, block in pieces] + [column_points, weights]
    if before:
        operands.append(tile)
    in_specs = [pl.BlockSpec(memory_space=pltpu.SMEM)] + [vmem] * (len(operands) - 1) + [hbm]
    operands.append(out)
    out_shape = [jax.ShapeDtypeStruct(out.shape, out.dtype)]
    out_specs = [hbm]
    scratch = []
    if last:
        scratch.append(pltpu.VMEM((rows, columns), jnp.float32))
    else:
        out_shape.append(jax.ShapeDtypeStruct((rows, columns), jnp.float32))
        out_specs.append(vmem)
    copies = len(before) + (len(chunks_of(places)) if last else 0)
    scratch.append(pltpu.SemaphoreType.DMA((max(copies, 1),)))
    result = pl.pallas_call(
        functools.partial(update_kernel, places, before, last, block_rows),
        out_shape=out_shape,
        in_specs=in_specs,
        out_specs=out_specs,
        scratch_shapes=scratch,
        input_output_aliases={len(operands) - 1: 0},
        compiler_params=pltpu.CompilerParams(vmem_limit_bytes=VMEM_BYTES),
        cost_estimate=pl.CostEstimate(flops=UPDATE_FLOPS, bytes_accessed=UPDATE_BYTES, transcendentals=0),
        name="update",
    )(*operands)
    if last:
        return result[0]
    return result[0], result[1], places


def fence(out):
    hbm = pl.BlockSpec(memory_space=pltpu.HBM)
    return pl.pallas_call(
        lambda held_ref, out_ref: None,
        out_shape=jax.ShapeDtypeStruct(out.shape, out.dtype),
        in_specs=[hbm],
        out_specs=hbm,
        input_output_aliases={0: 0},
        cost_estimate=pl.CostEstimate(flops=FENCE_FLOPS, bytes_accessed=0, transcendentals=0),
        name="fence",
    )(out)


def swapped(pieces, mask):
    pairs = [(i, i ^ mask) for i in range(lax.axis_size("col"))]
    return [(held ^ mask, row, lax.ppermute(block, "col", pairs)) for held, row, block in pieces]


def cut(pieces, row):
    first = [(mask, at, block[:row]) for mask, at, block in pieces]
    return first, [(mask, at + row, block[row:]) for mask, at, block in pieces]


def after(state, pieces):
    out, *blocks = lax.optimization_barrier((state[0], *[block for _, _, block in pieces]))
    return (out, *state[1:]), [(mask, row, block) for (mask, row, _), block in zip(pieces, blocks)]


def local(landmarks, slab_points, panel_points, inverse_blocks):
    size = lax.axis_size("col")
    rows = landmarks.shape[0]
    index = lax.axis_index("col").astype(jnp.int32).reshape(1)
    own = [(0, 0, landmarks)]
    bits = [1 << i for i in reversed(range(1, size.bit_length() - 1))]
    fresh = [swapped(half, bits[0]) for half in cut(own, rows // 16 * 8)]
    direct = [swapped(own, bit) for bit in bits[1:]]
    pending = own + swapped(own, 1)
    column_points, weights, out = setup(slab_points, panel_points, inverse_blocks, rows * size)
    state = (out, None, [])

    def computed(state, pieces, last=False):
        return update(state, index, rows, pieces, column_points, weights, last)

    moving = [[], []]
    for bit, close in zip(bits[1:], direct):
        state, first = after(state, fresh[0])
        moving[0] = moving[0] + first
        first_on = swapped(moving[0], bit)
        state = (fence(state[0]), *state[1:])
        near = swapped(first, 1)
        state = computed(state, pending)
        state = computed(state, first + near)

        state, second = after(state, fresh[1] + close)
        moving[1] = moving[1] + second[: len(fresh[1])]
        second_on = swapped(moving[1], bit)
        pending = swapped(second, 1)
        moving[1] = moving[1] + second[len(fresh[1]) :]
        state = (fence(state[0]), *state[1:])
        state = computed(state, second)
        fresh = [first_on, second_on]

    state, first = after(state, fresh[0])
    near = swapped(first, 1)
    state = computed(state, pending)
    state, second = after(state, fresh[1])
    far = swapped(second, 1)
    state = computed(state, first + near + second)
    return computed(state, far, last=True)


def solution(mesh):
    in_specs = (P(("row", "col"), None), P("col", None), P(), P())
    out_specs = P("row", "col")
    return jax.shard_map(local, mesh=mesh, in_specs=in_specs, out_specs=out_specs, check_vma=False)
```

time: 34.7 us -> 33.3 us (0.960)
  waiting for transfers between devices: 6.19 us -> 2.21 us
  local copies, waits for them, and re-layouts: 2.92 us -> 4.46 us
  Pallas kernels: 16.9 us -> 18 us
    ppermute x9 -> x11, waiting for transfers between devices: 6.19 us -> 2.21 us  [swapped(): lax.ppermute(block, 'col', pairs)]
    pallas_call x4 -> x8, Pallas kernels: 12.7 us -> 13.8 us  [the longest x6 13.8 us: update(): pl.pallas_call(functools.partial(update_kernel, places, before, last, blo...]
    slice x1, local copies, waits for them, and re-layouts: 0.02 us -> 1.02 us  [cut(): block[row:]]
    unnamed x8, local copies, waits for them, and re-layouts: 2.9 us -> 3.44 us
    ppermute x9 -> x11, starting transfers between devices: 8.29 us -> 8.22 us  [swapped(): lax.ppermute(block, 'col', pairs)]
  transfers between devices with their start and end apart: 9 -> 11, of which waited for: 3 -> 2; matrix products, arithmetic and copies ran while one was open for 0% -> 0% of each run, Pallas kernels for 45% -> 50%
where the time goes in v2:
time: 33.3 us; the launch traced here: 33 us
  Pallas kernels  18 us (54%)
  starting transfers between devices  8.22 us (25%)
  local copies, waits for them, and re-layouts  4.46 us (13%)
  waiting for transfers between devices  2.21 us (7%)
    pallas_call x6, Pallas kernels, update(): pl.pallas_call(functools.partial(update_kernel, places, before, last, blo...  13.8 us
    ppermute x11, starting transfers between devices, swapped(): lax.ppermute(block, 'col', pairs)  8.22 us
    pallas_call x1, Pallas kernels, setup(): pl.pallas_call(setup_kernel, out_shape=(jax.ShapeDtypeStruct((4 * dim, 2...  4.23 us
    unnamed x8, local copies, waits for them, and re-layouts  3.44 us
    ppermute x11, waiting for transfers between devices, swapped(): lax.ppermute(block, 'col', pairs)  2.21 us
    slice x1, local copies, waits for them, and re-layouts, cut(): block[row:]  1.02 us
  transfers between devices with their start and end apart: 11, of which 2 were waited for; matrix products, arithmetic and copies ran while one was open for 0% of the time, Pallas kernels for 50%

profile of v2, /device:TPU:0, one launch (start us, length us, event | category | flops | bytes accessed | tf_op | source)
XLA Modules:
  0.0 33.0 jit_solution(2943381283695008270)
XLA Ops:
  0.0 1.0 %fusion = (f32[320,128]{1,0:T(8,128)S(1)}, f32[320,128]{1,0:T(8,128)S(1)}) fusion(f32[640,128]{1,0:T(8,128)} %refs_1_.1), kind=kLoop, calls=%fused_computation | loop fusion | bytes 655360 | tf_op jit(solution)/shard_map/slice | solution.py:222
  1.0 4.1 %collective-permute-start = (f32[320,128]{1,0:T(8,128)S(1)}, f32[320,128]{1,0:T(8,128)S(1)}, u32[]{:S(2)}, u32[]{:S(2)}) collective-permute-start(f32[320,128]{1,0:T(8,128)S(1)} %get-tuple-element.50), channel_id=1, source_target_pairs={{0,4},{1,5},{2,6},{3,7},{4,0},{5,1},{6,2},{7,3},{8,12},{9,13},{10,... | collective-permute-start | bytes 491528 | tf_op jit(solution)/shard_map/ppermute | solution.py:217
  5.1 1.6 %collective-permute-start.4 = (f32[640,128]{1,0:T(8,128)}, f32[640,128]{1,0:T(8,128)S(1)}, u32[]{:S(2)}, u32[]{:S(2)}) collective-permute-start(f32[640,128]{1,0:T(8,128)} %refs_1_.1), channel_id=1, source_target_pairs={{0,2},{1,3},{2,0},{3,1},{4,6},{5,7},{6,4},{7,5},{8,10},{9,11},{10,... | collective-permute-start | bytes 983048 | tf_op jit(solution)/shard_map/ppermute | solution.py:217
  6.7 0.3 %collective-permute-start.3 = (f32[320,128]{1,0:T(8,128)S(1)}, f32[320,128]{1,0:T(8,128)S(1)}, u32[]{:S(2)}, u32[]{:S(2)}) collective-permute-start(f32[320,128]{1,0:T(8,128)S(1)} %get-tuple-element.49), channel_id=1, source_target_pairs={{0,4},{1,5},{2,6},{3,7},{4,0},{5,1},{6,2},{7,3},{8,12},{9,13},{10,... | collective-permute-start | bytes 491528 | tf_op jit(solution)/shard_map/ppermute | solution.py:217
  7.0 1.0 %copy-done.1 = f32[2,256,256]{2,1,0:T(8,128)S(1)} copy-done((f32[2,256,256]{2,1,0:T(8,128)S(1)}, f32[2,256,256]{2,1,0:T(8,128)}, u32[]{:S(2)}) %copy-start.1) | copy-done | bytes 524312
  8.1 0.9 %copy-done.2 = f32[2,256,128]{2,1,0:T(8,128)S(1)} copy-done((f32[2,256,128]{2,1,0:T(8,128)S(1)}, f32[2,256,128]{2,1,0:T(8,128)}, u32[]{:S(2)}) %copy-start.2) | copy-done | bytes 262168
  9.0 0.9 %copy-done.3 = f32[256,128]{1,0:T(8,128)S(1)} copy-done((f32[256,128]{1,0:T(8,128)S(1)}, f32[256,128]{1,0:T(8,128)}, u32[]{:S(2)}) %copy-start.3) | copy-done | bytes 131096
  9.9 4.2 %setup.1 = (bf16[512,768]{1,0:T(8,128)(2,1)S(1)}, bf16[1536,256]{1,0:T(8,128)(2,1)S(1)}, f32[5120,256]{1,0:T(8,128)}) custom-call(f32[256,128]{1,0:T(8,128)S(1)} %copy-done.3, f32[2,256,128]{2,1,0:T(8,128)S(1)} %copy-done.2, f32[2,256,256]{2,1,0:T(8,128)S(1)} %copy-done.1), custom_call_target="tpu_custom_call" | custom-call | flops 1700000000 | bytes 4194304 | tf_op jit(solution)/shard_map/setup/pallas_call | solution.py:87
  14.2 0.0 copy-start
  14.2 0.1 collective-permute-start.1
  14.3 0.3 %collective-permute-start.7 = (f32[320,128]{1,0:T(8,128)S(1)}, f32[320,128]{1,0:T(8,128)S(1)}, u32[]{:S(2)}, u32[]{:S(2)}) collective-permute-start(f32[320,128]{1,0:T(8,128)S(1)} %collective-permute-done.refs_1_), channel_id=1, source_target_pairs={{0,2},{1,3},{2,0},{3,1},{4,6},{5,7},{6,4},{7,5},{8,10},{9,11},{10,... | collective-permute-start | bytes 491528 | tf_op jit(solution)/shard_map/ppermute | solution.py:217
  14.6 0.5 %copy-done = f32[640,128]{1,0:T(8,128)S(1)} copy-done((f32[640,128]{1,0:T(8,128)S(1)}, f32[640,128]{1,0:T(8,128)}, u32[]{:S(2)}) %copy-start) | copy-done | bytes 327704
  15.2 2.4 %update.6 = (f32[5120,256]{1,0:T(8,128)}, f32[1280,256]{1,0:T(8,128)S(1)}) custom-call(s32[1]{0:T(128)} %bitcast.refs_0_, f32[640,128]{1,0:T(8,128)S(1)} %copy-done, f32[640,128]{1,0:T(8,128)S(1)} %collective-permute-done.2.refs_2_, bf16[512,768]{1,0:T(8,128)(2,1)S(1)} %get-tuple-element.29.refs_3_.refs_4_.refs_2_, ...), custom_call_target="tpu_custom_call", output_to_operand_aliasing={{0}: (5, {})} | custom-call | flops 1000000000 | bytes 10000000 | tf_op jit(solution)/shard_map/update/pallas_call | solution.py:186
  17.6 1.9 %update.7 = (f32[5120,256]{1,0:T(8,128)}, f32[640,256]{1,0:T(8,128)S(1)}) custom-call(s32[1]{0:T(128)} %bitcast.refs_0_, f32[320,128]{1,0:T(8,128)S(1)} %collective-permute-done.refs_1_, f32[320,128]{1,0:T(8,128)S(1)} %collective-permute-done.1.refs_2_, ...), custom_call_target="tpu_custom_call", output_to_operand_aliasing={{0}: (6, {})} | custom-call | flops 1000000000 | bytes 10000000 | tf_op jit(solution)/shard_map/update/pallas_call | solution.py:186
  19.5 0.7 %collective-permute-done.3.refs_1_ = f32[320,128]{1,0:T(8,128)S(1)} collective-permute-done((f32[320,128]{1,0:T(8,128)S(1)}, f32[320,128]{1,0:T(8,128)S(1)}, u32[]{:S(2)}, u32[]{:S(2)}) %collective-permute-start.3) | collective-permute-done | bytes 163872 | tf_op jit(solution)/shard_map/ppermute | solution.py:217
  20.2 1.5 %collective-permute-done.4.refs_2_ = f32[640,128]{1,0:T(8,128)S(1)} collective-permute-done((f32[640,128]{1,0:T(8,128)}, f32[640,128]{1,0:T(8,128)S(1)}, u32[]{:S(2)}, u32[]{:S(2)}) %collective-permute-start.4) | collective-permute-done | bytes 327712 | tf_op jit(solution)/shard_map/ppermute | solution.py:217
  21.7 0.9 %collective-permute-start.8 = (f32[320,128]{1,0:T(8,128)S(1)}, f32[320,128]{1,0:T(8,128)S(1)}, u32[]{:S(2)}, u32[]{:S(2)}) collective-permute-start(f32[320,128]{1,0:T(8,128)S(1)} %collective-permute-done.3.refs_1_), channel_id=1, source_target_pairs={{0,2},{1,3},{2,0},{3,1},{4,6},{5,7},{6,4},{7,5},{8,10},{9,11},{10,... | collective-permute-start | bytes 491528 | tf_op jit(solution)/shard_map/ppermute | solution.py:217
  22.6 0.2 collective-permute-start.6
  22.9 2.4 %update.8 = (f32[5120,256]{1,0:T(8,128)}, f32[960,256]{1,0:T(8,128)S(1)}) custom-call(s32[1]{0:T(128)} %bitcast.refs_0_, f32[320,128]{1,0:T(8,128)S(1)} %collective-permute-done.3.refs_1_, f32[640,128]{1,0:T(8,128)S(1)} %collective-permute-done.4.refs_2_, ...), custom_call_target="tpu_custom_call", output_to_operand_aliasing={{0}: (6, {})} | custom-call | flops 1000000000 | bytes 10000000 | tf_op jit(solution)/shard_map/update/pallas_call | solution.py:186
  25.3 0.3 %collective-permute-start.10 = (f32[320,128]{1,0:T(8,128)S(1)}, f32[320,128]{1,0:T(8,128)S(1)}, u32[]{:S(2)}, u32[]{:S(2)}) collective-permute-start(f32[320,128]{1,0:T(8,128)S(1)} %collective-permute-done.7.refs_1_), channel_id=1, source_target_pairs={{0,1},{1,0},{2,3},{3,2},{4,5},{5,4},{6,7},{7,6},{8,9},{9,8},{10,11... | collective-permute-start | bytes 491528 | tf_op jit(solution)/shard_map/ppermute | solution.py:217
  25.6 3.2 %update.9 = (f32[5120,256]{1,0:T(8,128)}, f32[960,256]{1,0:T(8,128)S(1)}) custom-call(s32[1]{0:T(128)} %bitcast.refs_0_, f32[320,128]{1,0:T(8,128)} %collective-permute-done.5.refs_1_, f32[640,128]{1,0:T(8,128)S(1)} %collective-permute-done.6.refs_2_, ...), custom_call_target="tpu_custom_call", output_to_operand_aliasing={{0}: (6, {})} | custom-call | flops 1000000000 | bytes 10000000 | tf_op jit(solution)/shard_map/update/pallas_call | solution.py:186
  28.8 0.3 collective-permute-start.9
  29.1 2.3 %update.10 = (f32[5120,256]{1,0:T(8,128)}, f32[960,256]{1,0:T(8,128)S(1)}) custom-call(s32[1]{0:T(128)} %bitcast.refs_0_, f32[320,128]{1,0:T(8,128)S(1)} %collective-permute-done.7.refs_1_, f32[320,128]{1,0:T(8,128)S(1)} %collective-permute-done.10.refs_2_, f32[320,128]{1,0:T(8,128)S(1)} %collective-permute-done.8.refs_3_, ...), custom_call_target="tpu_custom_call", output_to_operand_aliasing={{0}: (7, {})} | custom-call | flops 1000000000 | bytes 10000000 | tf_op jit(solution)/shard_map/update/pallas_call | solution.py:186
  31.4 1.6 %update.11 = f32[5120,256]{1,0:T(8,128)} custom-call(s32[1]{0:T(128)} %bitcast.refs_0_, f32[320,128]{1,0:T(8,128)S(1)} %collective-permute-done.9.refs_1_, bf16[512,768]{1,0:T(8,128)(2,1)S(1)} %get-tuple-element.29.refs_3_.refs_4_.refs_2_, bf16[1536,256]{1,0:T(8,128)(2,1)S(1)} %get-tuple-element.30.refs_4_.refs_5_.refs_3_, ...), custom_call_target="tpu_custom_call", output_to_operand_aliasing={{}: (5, {})} | custom-call | flops 1000000000 | bytes 10000000 | tf_op jit(solution)/shard_map/update/pallas_call | solution.py:186
  (16 shorter events, 0.0 us)
Async XLA Ops:
  1.0 13.2 %collective-permute-start = (f32[320,128]{1,0:T(8,128)S(1)}, f32[320,128]{1,0:T(8,128)S(1)}, u32[]{:S(2)}, u32[]{:S(2)}) collective-permute-start(f32[320,128]{1,0:T(8,128)S(1)} %get-tuple-element.50), channel_id=1, source_target_pairs={{0,4},{1,5},{2,6},{3,7},{4,0},{5,1},{6,2},{7,3},{8,12},{9,13},{10,... | collective-permute-start | bytes 491528 | tf_op jit(solution)/shard_map/ppermute | solution.py:217
  5.1 9.5 %collective-permute-start.2 = (f32[640,128]{1,0:T(8,128)}, f32[640,128]{1,0:T(8,128)S(1)}, u32[]{:S(2)}, u32[]{:S(2)}) collective-permute-start(f32[640,128]{1,0:T(8,128)} %refs_1_.1), channel_id=1, source_target_pairs={{0,1},{1,0},{2,3},{3,2},{4,5},{5,4},{6,7},{7,6},{8,9},{9,8},{10,11... | collective-permute-start | bytes 983048 | tf_op jit(solution)/shard_map/ppermute | solution.py:217
  5.1 16.6 %collective-permute-start.4 = (f32[640,128]{1,0:T(8,128)}, f32[640,128]{1,0:T(8,128)S(1)}, u32[]{:S(2)}, u32[]{:S(2)}) collective-permute-start(f32[640,128]{1,0:T(8,128)} %refs_1_.1), channel_id=1, source_target_pairs={{0,2},{1,3},{2,0},{3,1},{4,6},{5,7},{6,4},{7,5},{8,10},{9,11},{10,... | collective-permute-start | bytes 983048 | tf_op jit(solution)/shard_map/ppermute | solution.py:217
  6.7 13.5 %collective-permute-start.3 = (f32[320,128]{1,0:T(8,128)S(1)}, f32[320,128]{1,0:T(8,128)S(1)}, u32[]{:S(2)}, u32[]{:S(2)}) collective-permute-start(f32[320,128]{1,0:T(8,128)S(1)} %get-tuple-element.49), channel_id=1, source_target_pairs={{0,4},{1,5},{2,6},{3,7},{4,0},{5,1},{6,2},{7,3},{8,12},{9,13},{10,... | collective-permute-start | bytes 491528 | tf_op jit(solution)/shard_map/ppermute | solution.py:217
  7.0 1.0 %copy-start.1 = (f32[2,256,256]{2,1,0:T(8,128)S(1)}, f32[2,256,256]{2,1,0:T(8,128)}, u32[]{:S(2)}) copy-start(f32[2,256,256]{2,1,0:T(8,128)} %inverse_hbm.1) | copy-start | bytes 1572868
  8.1 0.9 %copy-start.2 = (f32[2,256,128]{2,1,0:T(8,128)S(1)}, f32[2,256,128]{2,1,0:T(8,128)}, u32[]{:S(2)}) copy-start(f32[2,256,128]{2,1,0:T(8,128)} %panel_hbm.1) | copy-start | bytes 786436
  9.0 0.9 %copy-start.3 = (f32[256,128]{1,0:T(8,128)S(1)}, f32[256,128]{1,0:T(8,128)}, u32[]{:S(2)}) copy-start(f32[256,128]{1,0:T(8,128)} %slab_hbm.1) | copy-start | bytes 393220
  14.2 1.0 %copy-start = (f32[640,128]{1,0:T(8,128)S(1)}, f32[640,128]{1,0:T(8,128)}, u32[]{:S(2)}) copy-start(f32[640,128]{1,0:T(8,128)} %refs_1_.1) | copy-start | bytes 983044
  14.2 3.4 %collective-permute-start.1 = (f32[320,128]{1,0:T(8,128)S(1)}, f32[320,128]{1,0:T(8,128)S(1)}, u32[]{:S(2)}, u32[]{:S(2)}) collective-permute-start(f32[320,128]{1,0:T(8,128)S(1)} %collective-permute-done.refs_1_), channel_id=1, source_target_pairs={{0,1},{1,0},{2,3},{3,2},{4,5},{5,4},{6,7},{7,6},{8,9},{9,8},{10,11... | collective-permute-start | bytes 491528 | tf_op jit(solution)/shard_map/ppermute | solution.py:217
  14.3 11.0 %collective-permute-start.7 = (f32[320,128]{1,0:T(8,128)S(1)}, f32[320,128]{1,0:T(8,128)S(1)}, u32[]{:S(2)}, u32[]{:S(2)}) collective-permute-start(f32[320,128]{1,0:T(8,128)S(1)} %collective-permute-done.refs_1_), channel_id=1, source_target_pairs={{0,2},{1,3},{2,0},{3,1},{4,6},{5,7},{6,4},{7,5},{8,10},{9,11},{10,... | collective-permute-start | bytes 491528 | tf_op jit(solution)/shard_map/ppermute | solution.py:217
  21.7 3.9 %collective-permute-start.5 = (f32[320,128]{1,0:T(8,128)S(1)}, f32[320,128]{1,0:T(8,128)}, u32[]{:S(2)}, u32[]{:S(2)}) collective-permute-start(f32[320,128]{1,0:T(8,128)S(1)} %collective-permute-done.3.refs_1_), channel_id=1, source_target_pairs={{0,1},{1,0},{2,3},{3,2},{4,5},{5,4},{6,7},{7,6},{8,9},{9,8},{10,11... | collective-permute-start | bytes 491528 | tf_op jit(solution)/shard_map/ppermute | solution.py:217
  21.7 7.1 %collective-permute-start.8 = (f32[320,128]{1,0:T(8,128)S(1)}, f32[320,128]{1,0:T(8,128)S(1)}, u32[]{:S(2)}, u32[]{:S(2)}) collective-permute-start(f32[320,128]{1,0:T(8,128)S(1)} %collective-permute-done.3.refs_1_), channel_id=1, source_target_pairs={{0,2},{1,3},{2,0},{3,1},{4,6},{5,7},{6,4},{7,5},{8,10},{9,11},{10,... | collective-permute-start | bytes 491528 | tf_op jit(solution)/shard_map/ppermute | solution.py:217
  22.6 3.0 %collective-permute-start.6 = (f32[640,128]{1,0:T(8,128)S(1)}, f32[640,128]{1,0:T(8,128)S(1)}, u32[]{:S(2)}, u32[]{:S(2)}) collective-permute-start(f32[640,128]{1,0:T(8,128)S(1)} %collective-permute-done.4.refs_2_), channel_id=1, source_target_pairs={{0,1},{1,0},{2,3},{3,2},{4,5},{5,4},{6,7},{7,6},{8,9},{9,8},{10,11... | collective-permute-start | bytes 983048 | tf_op jit(solution)/shard_map/ppermute | solution.py:217
  25.3 3.9 %collective-permute-start.10 = (f32[320,128]{1,0:T(8,128)S(1)}, f32[320,128]{1,0:T(8,128)S(1)}, u32[]{:S(2)}, u32[]{:S(2)}) collective-permute-start(f32[320,128]{1,0:T(8,128)S(1)} %collective-permute-done.7.refs_1_), channel_id=1, source_target_pairs={{0,1},{1,0},{2,3},{3,2},{4,5},{5,4},{6,7},{7,6},{8,9},{9,8},{10,11... | collective-permute-start | bytes 491528 | tf_op jit(solution)/shard_map/ppermute | solution.py:217
  28.8 2.6 %collective-permute-start.9 = (f32[320,128]{1,0:T(8,128)S(1)}, f32[320,128]{1,0:T(8,128)S(1)}, u32[]{:S(2)}, u32[]{:S(2)}) collective-permute-start(f32[320,128]{1,0:T(8,128)S(1)} %collective-permute-done.8.refs_3_), channel_id=1, source_target_pairs={{0,1},{1,0},{2,3},{3,2},{4,5},{5,4},{6,7},{7,6},{8,9},{9,8},{10,11... | collective-permute-start | bytes 491528 | tf_op jit(solution)/shard_map/ppermute | solution.py:217

commit v3 on v2

--- a/solution.py
+++ b/solution.py
@@ -12,7 +12,7 @@
 CHUNK = 160
 VMEM_BYTES = 16 << 20
 SETUP_FLOPS = 17 * 10**8
-UPDATE_FLOPS = 10**9
+UPDATE_FLOPS = 10**10
 UPDATE_BYTES = 10**7
 FENCE_FLOPS = 10**10
 
@@ -84,6 +84,7 @@
     panel = panel_points.shape[1]
     vmem = pl.BlockSpec(memory_space=pltpu.VMEM)
     operands = (slab_points, panel_points, inverse_blocks)
+    operands = [pltpu.with_memory_space_constraint(x, pltpu.HBM) for x in operands]
     return pl.pallas_call(
         setup_kernel,
         out_shape=(
@@ -123,7 +124,7 @@
     return chunks
 
 
-def update_kernel(places, before, last, block_rows, *refs):
+def update_kernel(places, before, now, block_rows, *refs):
     index_ref, refs = refs[0], refs[1:]
     blocks, (points_ref, weights_ref) = refs[: len(places)], refs[len(places) : len(places) + 2]
     me = index_ref[0]
@@ -155,13 +156,13 @@
             blocks[piece][used : used + size, :], points_ref[...], weights_ref[...]
         )
         used += size
-        if last:
+        if now:
             send(tile_ref, chunk)
     for copy in copies:
         copy.wait()
 
 
-def update(state, index, block_rows, pieces, column_points, weights, last=False):
+def update(state, index, block_rows, pieces, column_points, weights, now=False):
     out, tile, before = state
     places = [(mask, first_row, block.shape[0]) for mask, first_row, block in pieces]
     rows = sum(place[2] for place in places)
@@ -176,15 +177,15 @@
     out_shape = [jax.ShapeDtypeStruct(out.shape, out.dtype)]
     out_specs = [hbm]
     scratch = []
-    if last:
+    if now:
         scratch.append(pltpu.VMEM((rows, columns), jnp.float32))
     else:
         out_shape.append(jax.ShapeDtypeStruct((rows, columns), jnp.float32))
         out_specs.append(vmem)
-    copies = len(before) + (len(chunks_of(places)) if last else 0)
+    copies = len(before) + (len(chunks_of(places)) if now else 0)
     scratch.append(pltpu.SemaphoreType.DMA((max(copies, 1),)))
     result = pl.pallas_call(
-        functools.partial(update_kernel, places, before, last, block_rows),
+        functools.partial(update_kernel, places, before, now, block_rows),
         out_shape=out_shape,
         in_specs=in_specs,
         out_specs=out_specs,
@@ -194,9 +195,37 @@
         cost_estimate=pl.CostEstimate(flops=UPDATE_FLOPS, bytes_accessed=UPDATE_BYTES, transcendentals=0),
         name="update",
     )(*operands)
-    if last:
-        return result[0]
+    if now:
+        return result[0], None, []
     return result[0], result[1], places
+
+
+def parts_kernel(rows_hbm, first_ref, second_ref, sems):
+    half = first_ref.shape[0]
+    copies = [
+        pltpu.make_async_copy(rows_hbm.at[pl.ds(0, half), :], first_ref, sems.at[0]),
+        pltpu.make_async_copy(rows_hbm.at[pl.ds(half, second_ref.shape[0]), :], second_ref, sems.at[1]),
+    ]
+    for copy in copies:
+        copy.start()
+    for copy in copies:
+        copy.wait()
+
+
+def parts(rows, half):
+    vmem = pl.BlockSpec(memory_space=pltpu.VMEM)
+    count, dim = rows.shape
+    shapes = ((half, dim), (count - half, dim))
+    return pl.pallas_call(
+        parts_kernel,
+        out_shape=tuple(jax.ShapeDtypeStruct(shape, rows.dtype) for shape in shapes),
+        in_specs=[pl.BlockSpec(memory_space=pltpu.HBM)],
+        out_specs=(vmem, vmem),
+        scratch_shapes=[pltpu.SemaphoreType.DMA((2,))],
+        compiler_params=pltpu.CompilerParams(vmem_limit_bytes=VMEM_BYTES),
+        cost_estimate=pl.CostEstimate(flops=0, bytes_accessed=10**6, transcendentals=0),
+        name="parts",
+    )(pltpu.with_memory_space_constraint(rows, pltpu.HBM))
 
 
 def fence(out):
@@ -217,57 +246,62 @@
     return [(held ^ mask, row, lax.ppermute(block, "col", pairs)) for held, row, block in pieces]
 
 
-def cut(pieces, row):
-    first = [(mask, at, block[:row]) for mask, at, block in pieces]
-    return first, [(mask, at + row, block[row:]) for mask, at, block in pieces]
-
-
 def after(state, pieces):
     out, *blocks = lax.optimization_barrier((state[0], *[block for _, _, block in pieces]))
     return (out, *state[1:]), [(mask, row, block) for (mask, row, _), block in zip(pieces, blocks)]
 
 
+def fenced(state):
+    return (fence(state[0]), *state[1:])
+
+
 def local(landmarks, slab_points, panel_points, inverse_blocks):
     size = lax.axis_size("col")
     rows = landmarks.shape[0]
+    half = rows // 16 * 8
     index = lax.axis_index("col").astype(jnp.int32).reshape(1)
     own = [(0, 0, landmarks)]
+    upper, lower = parts(landmarks, half)
+    halves = [(0, 0, upper)], [(0, half, lower)]
     bits = [1 << i for i in reversed(range(1, size.bit_length() - 1))]
-    fresh = [swapped(half, bits[0]) for half in cut(own, rows // 16 * 8)]
+    fresh = [swapped(pieces, bits[0]) for pieces in halves]
     direct = [swapped(own, bit) for bit in bits[1:]]
-    pending = own + swapped(own, 1)
+    near_own = swapped(own, 1)
     column_points, weights, out = setup(slab_points, panel_points, inverse_blocks, rows * size)
     state = (out, None, [])
 
-    def computed(state, pieces, last=False):
-        return update(state, index, rows, pieces, column_points, weights, last)
+    def computed(state, pieces, now=False):
+        return update(state, index, rows, pieces, column_points, weights, now)
 
     moving = [[], []]
+    pending = halves[0] + halves[1] + near_own
     for bit, close in zip(bits[1:], direct):
         state, first = after(state, fresh[0])
         moving[0] = moving[0] + first
         first_on = swapped(moving[0], bit)
-        state = (fence(state[0]), *state[1:])
+        state = fenced(state)
         near = swapped(first, 1)
-        state = computed(state, pending)
-        state = computed(state, first + near)
-
-        state, second = after(state, fresh[1] + close)
-        moving[1] = moving[1] + second[: len(fresh[1])]
+        state = computed(state, pending, now=True)
+        state = computed(state, first + near, now=True)
+
+        state, second = after(state, fresh[1])
+        moving[1] = moving[1] + second
         second_on = swapped(moving[1], bit)
-        pending = swapped(second, 1)
-        moving[1] = moving[1] + second[len(fresh[1]) :]
-        state = (fence(state[0]), *state[1:])
-        state = computed(state, second)
+        near = swapped(second, 1)
+        state = fenced(state)
+        state, close = after(state, close)
+        moving[1] = moving[1] + close
+        pending = near + swapped(close, 1)
+        state = computed(state, second + close)
         fresh = [first_on, second_on]
 
     state, first = after(state, fresh[0])
     near = swapped(first, 1)
-    state = computed(state, pending)
+    state = computed(state, pending + first)
     state, second = after(state, fresh[1])
     far = swapped(second, 1)
-    state = computed(state, first + near + second)
-    return computed(state, far, last=True)
+    state = computed(state, second)
+    return computed(state, near + far, now=True)[0]
 
 
 def solution(mesh):

time: 33.3 us -> 32 us (0.961)
  local copies, waits for them, and re-layouts: 4.46 us -> 0 us
  Pallas kernels: 18 us -> 19.4 us
  starting transfers between devices: 8.22 us -> 9.42 us
  waiting for transfers between devices: 2.21 us -> 2.82 us
    unnamed x8 -> x0, local copies, waits for them, and re-layouts: 3.44 us -> none
    ppermute x11, starting transfers between devices: 8.22 us -> 9.42 us  [swapped(): lax.ppermute(block, 'col', pairs)]
    slice x1 -> x0, local copies, waits for them, and re-layouts: 1.02 us -> none  [cut(): block[row:]]
    pallas_call x1, Pallas kernels: 4.23 us -> 5.19 us  [setup(): pl.pallas_call(setup_kernel, out_shape=(jax.ShapeDtypeStruct((4 * dim, 2...]
    ppermute x11, waiting for transfers between devices: 2.21 us -> 2.82 us  [swapped(): lax.ppermute(block, 'col', pairs)]
    pallas_call x6 -> x7, Pallas kernels: 13.8 us -> 14.2 us  [the longest x6 13.2 us: update(): pl.pallas_call(functools.partial(update_kernel, places, before, now, bloc...]
  transfers between devices with their start and end apart: 11 -> 11, of which waited for: 2 -> 3; matrix products, arithmetic and copies ran while one was open for 0% -> 0% of each run, Pallas kernels for 50% -> 51%
where the time goes in v3:
time: 32 us; the launch traced here: 31.8 us
  Pallas kernels  19.4 us (61%)
  starting transfers between devices  9.42 us (29%)
  waiting for transfers between devices  2.82 us (9%)
    pallas_call x6, Pallas kernels, update(): pl.pallas_call(functools.partial(update_kernel, places, before, now, bloc...  13.2 us
    ppermute x11, starting transfers between devices, swapped(): lax.ppermute(block, 'col', pairs)  9.42 us
    pallas_call x1, Pallas kernels, setup(): pl.pallas_call(setup_kernel, out_shape=(jax.ShapeDtypeStruct((4 * dim, 2...  5.19 us
    ppermute x11, waiting for transfers between devices, swapped(): lax.ppermute(block, 'col', pairs)  2.82 us
    pallas_call x1, Pallas kernels, parts(): pl.pallas_call(parts_kernel, out_shape=tuple((jax.ShapeDtypeStruct(shape,...  1.01 us
  transfers between devices with their start and end apart: 11, of which 3 were waited for; matrix products, arithmetic and copies ran while one was open for 0% of the time, Pallas kernels for 51%

profile of v3, /device:TPU:0, one launch (start us, length us, event | category | flops | bytes accessed | tf_op | source)
XLA Modules:
  0.0 31.8 jit_solution(3652996458038507560)
XLA Ops:
  0.0 1.0 %parts.1 = (f32[320,128]{1,0:T(8,128)S(1)}, f32[320,128]{1,0:T(8,128)S(1)}) custom-call(f32[640,128]{1,0:T(8,128)} %rows_hbm.1), custom_call_target="tpu_custom_call" | custom-call | bytes 1000000 | tf_op jit(solution)/shard_map/parts/pallas_call | solution.py:219
  1.0 4.1 %collective-permute-start = (f32[320,128]{1,0:T(8,128)S(1)}, f32[320,128]{1,0:T(8,128)S(1)}, u32[]{:S(2)}, u32[]{:S(2)}) collective-permute-start(f32[320,128]{1,0:T(8,128)S(1)} %get-tuple-element.27.refs_1_), channel_id=1, source_target_pairs={{0,4},{1,5},{2,6},{3,7},{4,0},{5,1},{6,2},{7,3},{8,12},{9,13},{10,... | collective-permute-start | bytes 491528 | tf_op jit(solution)/shard_map/ppermute | solution.py:246
  5.1 1.6 %collective-permute-start.4 = (f32[640,128]{1,0:T(8,128)}, f32[640,128]{1,0:T(8,128)S(1)}, u32[]{:S(2)}, u32[]{:S(2)}) collective-permute-start(f32[640,128]{1,0:T(8,128)} %rows_hbm.1), channel_id=1, source_target_pairs={{0,2},{1,3},{2,0},{3,1},{4,6},{5,7},{6,4},{7,5},{8,10},{9,11},{10,... | collective-permute-start | bytes 983048 | tf_op jit(solution)/shard_map/ppermute | solution.py:246
  6.7 0.0 collective-permute-start.2
  6.7 0.3 %collective-permute-start.3 = (f32[320,128]{1,0:T(8,128)S(1)}, f32[320,128]{1,0:T(8,128)S(1)}, u32[]{:S(2)}, u32[]{:S(2)}) collective-permute-start(f32[320,128]{1,0:T(8,128)S(1)} %get-tuple-element.31.refs_2_), channel_id=1, source_target_pairs={{0,4},{1,5},{2,6},{3,7},{4,0},{5,1},{6,2},{7,3},{8,12},{9,13},{10,... | collective-permute-start | bytes 491528 | tf_op jit(solution)/shard_map/ppermute | solution.py:246
  7.0 5.2 %setup.1 = (bf16[512,768]{1,0:T(8,128)(2,1)S(1)}, bf16[1536,256]{1,0:T(8,128)(2,1)S(1)}, f32[5120,256]{1,0:T(8,128)}) custom-call(f32[256,128]{1,0:T(8,128)} %slab_hbm.1, f32[2,256,128]{2,1,0:T(8,128)} %panel_hbm.1, f32[2,256,256]{2,1,0:T(8,128)} %inverse_hbm.1), custom_call_target="tpu_custom_call" | custom-call | flops 1700000000 | bytes 4194304 | tf_op jit(solution)/shard_map/setup/pallas_call | solution.py:88
  12.2 1.5 %collective-permute-done.refs_1_ = f32[320,128]{1,0:T(8,128)S(1)} collective-permute-done((f32[320,128]{1,0:T(8,128)S(1)}, f32[320,128]{1,0:T(8,128)S(1)}, u32[]{:S(2)}, u32[]{:S(2)}) %collective-permute-start) | collective-permute-done | bytes 163872 | tf_op jit(solution)/shard_map/ppermute | solution.py:246
  13.8 0.0 collective-permute-start.5
  13.8 0.0 collective-permute-start.1
  13.8 0.0 collective-permute-done.2.refs_3_
  13.8 3.2 %update.6.refs_5_ = f32[5120,256]{1,0:T(8,128)} custom-call(s32[1]{0:T(128)} %bitcast.refs_0_, f32[320,128]{1,0:T(8,128)S(1)} %get-tuple-element.27.refs_1_, f32[320,128]{1,0:T(8,128)S(1)} %get-tuple-element.31.refs_2_, f32[640,128]{1,0:T(8,128)S(1)} %collective-permute-done.2.refs_3_, ...), custom_call_target="tpu_custom_call", output_to_operand_aliasing={{}: (6, {})} | custom-call | flops 10000000000 | bytes 10000000 | tf_op jit(solution)/shard_map/update/pallas_call | solution.py:187
  17.0 2.1 %update.7.held_ref = f32[5120,256]{1,0:T(8,128)} custom-call(s32[1]{0:T(128)} %bitcast.refs_0_, f32[320,128]{1,0:T(8,128)S(1)} %collective-permute-done.refs_1_, f32[320,128]{1,0:T(8,128)S(1)} %collective-permute-done.1.refs_2_, bf16[512,768]{1,0:T(8,128)(2,1)S(1)} %get-tuple-element.29.refs_4_.refs_3_.refs_2_, ...), custom_call_target="tpu_custom_call", output_to_operand_aliasing={{}: (5, {})} | custom-call | flops 10000000000 | bytes 10000000 | tf_op jit(solution)/shard_map/update/pallas_call | solution.py:187
  19.1 1.2 %collective-permute-done.3.refs_1_ = f32[320,128]{1,0:T(8,128)S(1)} collective-permute-done((f32[320,128]{1,0:T(8,128)S(1)}, f32[320,128]{1,0:T(8,128)S(1)}, u32[]{:S(2)}, u32[]{:S(2)}) %collective-permute-start.3) | collective-permute-done | bytes 163872 | tf_op jit(solution)/shard_map/ppermute | solution.py:246
  20.3 2.3 %collective-permute-start.9 = (f32[320,128]{1,0:T(8,128)S(1)}, f32[320,128]{1,0:T(8,128)S(1)}, u32[]{:S(2)}, u32[]{:S(2)}) collective-permute-start(f32[320,128]{1,0:T(8,128)S(1)} %collective-permute-done.3.refs_1_), channel_id=1, source_target_pairs={{0,2},{1,3},{2,0},{3,1},{4,6},{5,7},{6,4},{7,5},{8,10},{9,11},{10,... | collective-permute-start | bytes 491528 | tf_op jit(solution)/shard_map/ppermute | solution.py:246
  22.6 0.0 collective-permute-done.4.refs_2_
  22.6 0.5 %collective-permute-start.8 = (f32[640,128]{1,0:T(8,128)S(1)}, f32[640,128]{1,0:T(8,128)S(1)}, u32[]{:S(2)}, u32[]{:S(2)}) collective-permute-start(f32[640,128]{1,0:T(8,128)S(1)} %collective-permute-done.4.refs_2_), channel_id=1, source_target_pairs={{0,1},{1,0},{2,3},{3,2},{4,5},{5,4},{6,7},{7,6},{8,9},{9,8},{10,11... | collective-permute-start | bytes 983048 | tf_op jit(solution)/shard_map/ppermute | solution.py:246
  23.1 1.9 %update.8 = (f32[5120,256]{1,0:T(8,128)}, f32[960,256]{1,0:T(8,128)S(1)}) custom-call(s32[1]{0:T(128)} %bitcast.refs_0_, f32[320,128]{1,0:T(8,128)S(1)} %collective-permute-done.3.refs_1_, f32[640,128]{1,0:T(8,128)S(1)} %collective-permute-done.4.refs_2_, ...), custom_call_target="tpu_custom_call", output_to_operand_aliasing={{0}: (5, {})} | custom-call | flops 10000000000 | bytes 10000000 | tf_op jit(solution)/shard_map/update/pallas_call | solution.py:187
  25.1 0.1 collective-permute-done.5.refs_3_
  25.1 0.0 collective-permute-start.6
  25.2 0.0 collective-permute-done.7.refs_1_
  25.2 2.8 %update.9 = (f32[5120,256]{1,0:T(8,128)}, f32[1280,256]{1,0:T(8,128)S(1)}) custom-call(s32[1]{0:T(128)} %bitcast.refs_0_, f32[320,128]{1,0:T(8,128)S(1)} %collective-permute-done.7.refs_1_, f32[640,128]{1,0:T(8,128)S(1)} %collective-permute-done.8.refs_2_, f32[320,128]{1,0:T(8,128)S(1)} %collective-permute-done.5.refs_3_, ...), custom_call_target="tpu_custom_call", output_to_operand_aliasing={{0}: (7, {})} | custom-call | flops 10000000000 | bytes 10000000 | tf_op jit(solution)/shard_map/update/pallas_call | solution.py:187
  28.0 0.5 %collective-permute-start.10 = (f32[320,128]{1,0:T(8,128)S(1)}, f32[320,128]{1,0:T(8,128)S(1)}, u32[]{:S(2)}, u32[]{:S(2)}) collective-permute-start(f32[320,128]{1,0:T(8,128)S(1)} %collective-permute-done.9.refs_1_), channel_id=1, source_target_pairs={{0,1},{1,0},{2,3},{3,2},{4,5},{5,4},{6,7},{7,6},{8,9},{9,8},{10,11... | collective-permute-start | bytes 491528 | tf_op jit(solution)/shard_map/ppermute | solution.py:246
  28.6 1.1 %update.10 = (f32[5120,256]{1,0:T(8,128)}, f32[320,256]{1,0:T(8,128)S(1)}) custom-call(s32[1]{0:T(128)} %bitcast.refs_0_, f32[320,128]{1,0:T(8,128)S(1)} %collective-permute-done.9.refs_1_, bf16[512,768]{1,0:T(8,128)(2,1)S(1)} %get-tuple-element.29.refs_4_.refs_3_.refs_2_, ...), custom_call_target="tpu_custom_call", output_to_operand_aliasing={{0}: (5, {})} | custom-call | flops 10000000000 | bytes 10000000 | tf_op jit(solution)/shard_map/update/pallas_call | solution.py:187
  29.7 2.1 %update.11 = f32[5120,256]{1,0:T(8,128)} custom-call(s32[1]{0:T(128)} %bitcast.refs_0_, f32[320,128]{1,0:T(8,128)S(1)} %collective-permute-done.6.refs_1_, f32[320,128]{1,0:T(8,128)S(1)} %collective-permute-done.10.refs_2_, bf16[512,768]{1,0:T(8,128)(2,1)S(1)} %get-tuple-element.29.refs_4_.refs_3_.refs_2_, ...), custom_call_target="tpu_custom_call", output_to_operand_aliasing={{}: (6, {})} | custom-call | flops 10000000000 | bytes 10000000 | tf_op jit(solution)/shard_map/update/pallas_call | solution.py:187
  (8 shorter events, 0.0 us)
Async XLA Ops:
  1.0 12.7 %collective-permute-start = (f32[320,128]{1,0:T(8,128)S(1)}, f32[320,128]{1,0:T(8,128)S(1)}, u32[]{:S(2)}, u32[]{:S(2)}) collective-permute-start(f32[320,128]{1,0:T(8,128)S(1)} %get-tuple-element.27.refs_1_), channel_id=1, source_target_pairs={{0,4},{1,5},{2,6},{3,7},{4,0},{5,1},{6,2},{7,3},{8,12},{9,13},{10,... | collective-permute-start | bytes 491528 | tf_op jit(solution)/shard_map/ppermute | solution.py:246
  5.1 17.5 %collective-permute-start.4 = (f32[640,128]{1,0:T(8,128)}, f32[640,128]{1,0:T(8,128)S(1)}, u32[]{:S(2)}, u32[]{:S(2)}) collective-permute-start(f32[640,128]{1,0:T(8,128)} %rows_hbm.1), channel_id=1, source_target_pairs={{0,2},{1,3},{2,0},{3,1},{4,6},{5,7},{6,4},{7,5},{8,10},{9,11},{10,... | collective-permute-start | bytes 983048 | tf_op jit(solution)/shard_map/ppermute | solution.py:246
  6.7 7.1 %collective-permute-start.2 = (f32[640,128]{1,0:T(8,128)}, f32[640,128]{1,0:T(8,128)S(1)}, u32[]{:S(2)}, u32[]{:S(2)}) collective-permute-start(f32[640,128]{1,0:T(8,128)} %rows_hbm.1), channel_id=1, source_target_pairs={{0,1},{1,0},{2,3},{3,2},{4,5},{5,4},{6,7},{7,6},{8,9},{9,8},{10,11... | collective-permute-start | bytes 983048 | tf_op jit(solution)/shard_map/ppermute | solution.py:246
  6.7 13.6 %collective-permute-start.3 = (f32[320,128]{1,0:T(8,128)S(1)}, f32[320,128]{1,0:T(8,128)S(1)}, u32[]{:S(2)}, u32[]{:S(2)}) collective-permute-start(f32[320,128]{1,0:T(8,128)S(1)} %get-tuple-element.31.refs_2_), channel_id=1, source_target_pairs={{0,4},{1,5},{2,6},{3,7},{4,0},{5,1},{6,2},{7,3},{8,12},{9,13},{10,... | collective-permute-start | bytes 491528 | tf_op jit(solution)/shard_map/ppermute | solution.py:246
  13.8 11.4 %collective-permute-start.5 = (f32[320,128]{1,0:T(8,128)S(1)}, f32[320,128]{1,0:T(8,128)S(1)}, u32[]{:S(2)}, u32[]{:S(2)}) collective-permute-start(f32[320,128]{1,0:T(8,128)S(1)} %collective-permute-done.refs_1_), channel_id=1, source_target_pairs={{0,2},{1,3},{2,0},{3,1},{4,6},{5,7},{6,4},{7,5},{8,10},{9,11},{10,... | collective-permute-start | bytes 491528 | tf_op jit(solution)/shard_map/ppermute | solution.py:246
  13.8 3.2 %collective-permute-start.1 = (f32[320,128]{1,0:T(8,128)S(1)}, f32[320,128]{1,0:T(8,128)S(1)}, u32[]{:S(2)}, u32[]{:S(2)}) collective-permute-start(f32[320,128]{1,0:T(8,128)S(1)} %collective-permute-done.refs_1_), channel_id=1, source_target_pairs={{0,1},{1,0},{2,3},{3,2},{4,5},{5,4},{6,7},{7,6},{8,9},{9,8},{10,11... | collective-permute-start | bytes 491528 | tf_op jit(solution)/shard_map/ppermute | solution.py:246
  20.3 7.7 %collective-permute-start.9 = (f32[320,128]{1,0:T(8,128)S(1)}, f32[320,128]{1,0:T(8,128)S(1)}, u32[]{:S(2)}, u32[]{:S(2)}) collective-permute-start(f32[320,128]{1,0:T(8,128)S(1)} %collective-permute-done.3.refs_1_), channel_id=1, source_target_pairs={{0,2},{1,3},{2,0},{3,1},{4,6},{5,7},{6,4},{7,5},{8,10},{9,11},{10,... | collective-permute-start | bytes 491528 | tf_op jit(solution)/shard_map/ppermute | solution.py:246
  22.6 2.5 %collective-permute-start.7 = (f32[320,128]{1,0:T(8,128)S(1)}, f32[320,128]{1,0:T(8,128)S(1)}, u32[]{:S(2)}, u32[]{:S(2)}) collective-permute-start(f32[320,128]{1,0:T(8,128)S(1)} %collective-permute-done.3.refs_1_), channel_id=1, source_target_pairs={{0,1},{1,0},{2,3},{3,2},{4,5},{5,4},{6,7},{7,6},{8,9},{9,8},{10,11... | collective-permute-start | bytes 491528 | tf_op jit(solution)/shard_map/ppermute | solution.py:246
  22.6 2.5 %collective-permute-start.8 = (f32[640,128]{1,0:T(8,128)S(1)}, f32[640,128]{1,0:T(8,128)S(1)}, u32[]{:S(2)}, u32[]{:S(2)}) collective-permute-start(f32[640,128]{1,0:T(8,128)S(1)} %collective-permute-done.4.refs_2_), channel_id=1, source_target_pairs={{0,1},{1,0},{2,3},{3,2},{4,5},{5,4},{6,7},{7,6},{8,9},{9,8},{10,11... | collective-permute-start | bytes 983048 | tf_op jit(solution)/shard_map/ppermute | solution.py:246
  25.1 4.5 %collective-permute-start.6 = (f32[320,128]{1,0:T(8,128)S(1)}, f32[320,128]{1,0:T(8,128)S(1)}, u32[]{:S(2)}, u32[]{:S(2)}) collective-permute-start(f32[320,128]{1,0:T(8,128)S(1)} %collective-permute-done.5.refs_3_), channel_id=1, source_target_pairs={{0,1},{1,0},{2,3},{3,2},{4,5},{5,4},{6,7},{7,6},{8,9},{9,8},{10,11... | collective-permute-start | bytes 491528 | tf_op jit(solution)/shard_map/ppermute | solution.py:246
  28.0 1.7 %collective-permute-start.10 = (f32[320,128]{1,0:T(8,128)S(1)}, f32[320,128]{1,0:T(8,128)S(1)}, u32[]{:S(2)}, u32[]{:S(2)}) collective-permute-start(f32[320,128]{1,0:T(8,128)S(1)} %collective-permute-done.9.refs_1_), channel_id=1, source_target_pairs={{0,1},{1,0},{2,3},{3,2},{4,5},{5,4},{6,7},{7,6},{8,9},{9,8},{10,11... | collective-permute-start | bytes 491528 | tf_op jit(solution)/shard_map/ppermute | solution.py:246

commit v4 on v3

--- a/solution.py
+++ b/solution.py
@@ -156,8 +156,11 @@
             blocks[piece][used : used + size, :], points_ref[...], weights_ref[...]
         )
         used += size
-        if now:
+        mask, first_row, rows = places[piece]
+        if now and piece == len(places) - 1:
             send(tile_ref, chunk)
+        elif now and used == rows:
+            send(tile_ref, (first + size - rows, mask, first_row, rows))
     for copy in copies:
         copy.wait()
 
@@ -276,12 +279,12 @@
     moving = [[], []]
     pending = halves[0] + halves[1] + near_own
     for bit, close in zip(bits[1:], direct):
+        state = computed(state, pending, now=True)
         state, first = after(state, fresh[0])
         moving[0] = moving[0] + first
         first_on = swapped(moving[0], bit)
+        near = swapped(first, 1)
         state = fenced(state)
-        near = swapped(first, 1)
-        state = computed(state, pending, now=True)
         state = computed(state, first + near, now=True)
 
         state, second = after(state, fresh[1])

time: 32 us -> 31.9 us (level)
  transfers between devices with their start and end apart: 11 -> 11, of which waited for: 3 -> 4; matrix products, arithmetic and copies ran while one was open for 0% -> 0% of each run, Pallas kernels for 51% -> 55%
where the time goes in v4:
time: 31.9 us; the launch traced here: 31.7 us
  Pallas kernels  19.4 us (61%)
  starting transfers between devices  9.67 us (30%)
  waiting for transfers between devices  2.52 us (8%)
    pallas_call x6, Pallas kernels, update(): pl.pallas_call(functools.partial(update_kernel, places, before, now, bloc...  13.2 us
    ppermute x11, starting transfers between devices, swapped(): lax.ppermute(block, 'col', pairs)  9.67 us
    pallas_call x1, Pallas kernels, setup(): pl.pallas_call(setup_kernel, out_shape=(jax.ShapeDtypeStruct((4 * dim, 2...  5.19 us
    ppermute x11, waiting for transfers between devices, swapped(): lax.ppermute(block, 'col', pairs)  2.52 us
    pallas_call x1, Pallas kernels, parts(): pl.pallas_call(parts_kernel, out_shape=tuple((jax.ShapeDtypeStruct(shape,...  1.01 us
  transfers between devices with their start and end apart: 11, of which 4 were waited for; matrix products, arithmetic and copies ran while one was open for 0% of the time, Pallas kernels for 55%

profile of v4, /device:TPU:0, one launch (start us, length us, event | category | flops | bytes accessed | tf_op | source)
XLA Modules:
  0.0 31.7 jit_solution(1245574768405321517)
XLA Ops:
  0.0 0.5 %collective-permute-start = (f32[640,128]{1,0:T(8,128)}, f32[640,128]{1,0:T(8,128)S(1)}, u32[]{:S(2)}, u32[]{:S(2)}) collective-permute-start(f32[640,128]{1,0:T(8,128)} %rows_hbm.1), channel_id=1, source_target_pairs={{0,1},{1,0},{2,3},{3,2},{4,5},{5,4},{6,7},{7,6},{8,9},{9,8},{10,11... | collective-permute-start | bytes 983048 | tf_op jit(solution)/shard_map/ppermute | solution.py:249
  0.5 2.6 %collective-permute-start.4 = (f32[640,128]{1,0:T(8,128)}, f32[640,128]{1,0:T(8,128)S(1)}, u32[]{:S(2)}, u32[]{:S(2)}) collective-permute-start(f32[640,128]{1,0:T(8,128)} %rows_hbm.1), channel_id=1, source_target_pairs={{0,2},{1,3},{2,0},{3,1},{4,6},{5,7},{6,4},{7,5},{8,10},{9,11},{10,... | collective-permute-start | bytes 983048 | tf_op jit(solution)/shard_map/ppermute | solution.py:249
  3.0 1.0 %parts.1 = (f32[320,128]{1,0:T(8,128)S(1)}, f32[320,128]{1,0:T(8,128)S(1)}) custom-call(f32[640,128]{1,0:T(8,128)} %rows_hbm.1), custom_call_target="tpu_custom_call" | custom-call | bytes 1000000 | tf_op jit(solution)/shard_map/parts/pallas_call | solution.py:222
  4.0 2.7 %collective-permute-start.1 = (f32[320,128]{1,0:T(8,128)S(1)}, f32[320,128]{1,0:T(8,128)S(1)}, u32[]{:S(2)}, u32[]{:S(2)}) collective-permute-start(f32[320,128]{1,0:T(8,128)S(1)} %get-tuple-element.26.refs_1_), channel_id=1, source_target_pairs={{0,4},{1,5},{2,6},{3,7},{4,0},{5,1},{6,2},{7,3},{8,12},{9,13},{10,... | collective-permute-start | bytes 491528 | tf_op jit(solution)/shard_map/ppermute | solution.py:249
  6.7 0.3 %collective-permute-start.3 = (f32[320,128]{1,0:T(8,128)S(1)}, f32[320,128]{1,0:T(8,128)S(1)}, u32[]{:S(2)}, u32[]{:S(2)}) collective-permute-start(f32[320,128]{1,0:T(8,128)S(1)} %get-tuple-element.27.refs_2_), channel_id=1, source_target_pairs={{0,4},{1,5},{2,6},{3,7},{4,0},{5,1},{6,2},{7,3},{8,12},{9,13},{10,... | collective-permute-start | bytes 491528 | tf_op jit(solution)/shard_map/ppermute | solution.py:249
  7.0 5.2 %setup.1 = (bf16[512,768]{1,0:T(8,128)(2,1)S(1)}, bf16[1536,256]{1,0:T(8,128)(2,1)S(1)}, f32[5120,256]{1,0:T(8,128)}) custom-call(f32[256,128]{1,0:T(8,128)} %slab_hbm.1, f32[2,256,128]{2,1,0:T(8,128)} %panel_hbm.1, f32[2,256,256]{2,1,0:T(8,128)} %inverse_hbm.1), custom_call_target="tpu_custom_call" | custom-call | flops 1700000000 | bytes 4194304 | tf_op jit(solution)/shard_map/setup/pallas_call | solution.py:88
  12.2 0.0 collective-permute-done.refs_3_
  12.2 3.2 %update.6.held_ref = f32[5120,256]{1,0:T(8,128)} custom-call(s32[1]{0:T(128)} %bitcast.refs_0_, f32[320,128]{1,0:T(8,128)S(1)} %get-tuple-element.26.refs_1_, f32[320,128]{1,0:T(8,128)S(1)} %get-tuple-element.27.refs_2_, f32[640,128]{1,0:T(8,128)S(1)} %collective-permute-done.refs_3_, ...), custom_call_target="tpu_custom_call", output_to_operand_aliasing={{}: (6, {})} | custom-call | flops 10000000000 | bytes 10000000 | tf_op jit(solution)/shard_map/update/pallas_call | solution.py:190
  15.4 2.9 %collective-permute-start.5 = (f32[320,128]{1,0:T(8,128)S(1)}, f32[320,128]{1,0:T(8,128)S(1)}, u32[]{:S(2)}, u32[]{:S(2)}) collective-permute-start(f32[320,128]{1,0:T(8,128)S(1)} %collective-permute-done.1.refs_1_), channel_id=1, source_target_pairs={{0,2},{1,3},{2,0},{3,1},{4,6},{5,7},{6,4},{7,5},{8,10},{9,11},{10,... | collective-permute-start | bytes 491528 | tf_op jit(solution)/shard_map/ppermute | solution.py:249
  18.4 0.0 collective-permute-start.2
  18.4 1.4 %collective-permute-done.2.refs_2_ = f32[320,128]{1,0:T(8,128)S(1)} collective-permute-done((f32[320,128]{1,0:T(8,128)S(1)}, f32[320,128]{1,0:T(8,128)S(1)}, u32[]{:S(2)}, u32[]{:S(2)}) %collective-permute-start.2) | collective-permute-done | bytes 163872 | tf_op jit(solution)/shard_map/ppermute | solution.py:249
  19.8 2.1 %update.7.held_ref = f32[5120,256]{1,0:T(8,128)} custom-call(s32[1]{0:T(128)} %bitcast.refs_0_, f32[320,128]{1,0:T(8,128)S(1)} %collective-permute-done.1.refs_1_, f32[320,128]{1,0:T(8,128)S(1)} %collective-permute-done.2.refs_2_, bf16[512,768]{1,0:T(8,128)(2,1)S(1)} %get-tuple-element.28.refs_4_.refs_3_.refs_2_, ...), custom_call_target="tpu_custom_call", output_to_operand_aliasing={{}: (5, {})} | custom-call | flops 10000000000 | bytes 10000000 | tf_op jit(solution)/shard_map/update/pallas_call | solution.py:190
  21.9 0.2 collective-permute-done.3.refs_1_
  22.0 0.0 collective-permute-start.9
  22.0 0.1 collective-permute-start.7
  22.2 0.4 %collective-permute-start.8 = (f32[640,128]{1,0:T(8,128)S(1)}, f32[640,128]{1,0:T(8,128)S(1)}, u32[]{:S(2)}, u32[]{:S(2)}) collective-permute-start(f32[640,128]{1,0:T(8,128)S(1)} %collective-permute-done.4.refs_2_), channel_id=1, source_target_pairs={{0,1},{1,0},{2,3},{3,2},{4,5},{5,4},{6,7},{7,6},{8,9},{9,8},{10,11... | collective-permute-start | bytes 983048 | tf_op jit(solution)/shard_map/ppermute | solution.py:249
  22.5 1.9 %update.8 = (f32[5120,256]{1,0:T(8,128)}, f32[960,256]{1,0:T(8,128)S(1)}) custom-call(s32[1]{0:T(128)} %bitcast.refs_0_, f32[320,128]{1,0:T(8,128)S(1)} %collective-permute-done.3.refs_1_, f32[640,128]{1,0:T(8,128)S(1)} %collective-permute-done.4.refs_2_, ...), custom_call_target="tpu_custom_call", output_to_operand_aliasing={{0}: (5, {})} | custom-call | flops 10000000000 | bytes 10000000 | tf_op jit(solution)/shard_map/update/pallas_call | solution.py:190
  24.5 0.0 collective-permute-done.5.refs_3_
  24.5 0.2 collective-permute-start.6
  24.7 2.8 %update.9 = (f32[5120,256]{1,0:T(8,128)}, f32[1280,256]{1,0:T(8,128)S(1)}) custom-call(s32[1]{0:T(128)} %bitcast.refs_0_, f32[320,128]{1,0:T(8,128)S(1)} %collective-permute-done.7.refs_1_, f32[640,128]{1,0:T(8,128)S(1)} %collective-permute-done.8.refs_2_, f32[320,128]{1,0:T(8,128)S(1)} %collective-permute-done.5.refs_3_, ...), custom_call_target="tpu_custom_call", output_to_operand_aliasing={{0}: (7, {})} | custom-call | flops 10000000000 | bytes 10000000 | tf_op jit(solution)/shard_map/update/pallas_call | solution.py:190
  27.5 0.7 %collective-permute-done.9.refs_1_ = f32[320,128]{1,0:T(8,128)S(1)} collective-permute-done((f32[320,128]{1,0:T(8,128)S(1)}, f32[320,128]{1,0:T(8,128)S(1)}, u32[]{:S(2)}, u32[]{:S(2)}) %collective-permute-start.9) | collective-permute-done | bytes 163872 | tf_op jit(solution)/shard_map/ppermute | solution.py:249
  28.2 1.1 %update.10 = (f32[5120,256]{1,0:T(8,128)}, f32[320,256]{1,0:T(8,128)S(1)}) custom-call(s32[1]{0:T(128)} %bitcast.refs_0_, f32[320,128]{1,0:T(8,128)S(1)} %collective-permute-done.9.refs_1_, bf16[512,768]{1,0:T(8,128)(2,1)S(1)} %get-tuple-element.28.refs_4_.refs_3_.refs_2_, ...), custom_call_target="tpu_custom_call", output_to_operand_aliasing={{0}: (5, {})} | custom-call | flops 10000000000 | bytes 10000000 | tf_op jit(solution)/shard_map/update/pallas_call | solution.py:190
  29.3 0.3 collective-permute-done.10.refs_2_
  29.6 2.1 %update.11 = f32[5120,256]{1,0:T(8,128)} custom-call(s32[1]{0:T(128)} %bitcast.refs_0_, f32[320,128]{1,0:T(8,128)S(1)} %collective-permute-done.6.refs_1_, f32[320,128]{1,0:T(8,128)S(1)} %collective-permute-done.10.refs_2_, bf16[512,768]{1,0:T(8,128)(2,1)S(1)} %get-tuple-element.28.refs_4_.refs_3_.refs_2_, ...), custom_call_target="tpu_custom_call", output_to_operand_aliasing={{}: (6, {})} | custom-call | flops 10000000000 | bytes 10000000 | tf_op jit(solution)/shard_map/update/pallas_call | solution.py:190
  (8 shorter events, 0.0 us)
Async XLA Ops:
  0.0 12.2 %collective-permute-start = (f32[640,128]{1,0:T(8,128)}, f32[640,128]{1,0:T(8,128)S(1)}, u32[]{:S(2)}, u32[]{:S(2)}) collective-permute-start(f32[640,128]{1,0:T(8,128)} %rows_hbm.1), channel_id=1, source_target_pairs={{0,1},{1,0},{2,3},{3,2},{4,5},{5,4},{6,7},{7,6},{8,9},{9,8},{10,11... | collective-permute-start | bytes 983048 | tf_op jit(solution)/shard_map/ppermute | solution.py:249
  0.5 21.7 %collective-permute-start.4 = (f32[640,128]{1,0:T(8,128)}, f32[640,128]{1,0:T(8,128)S(1)}, u32[]{:S(2)}, u32[]{:S(2)}) collective-permute-start(f32[640,128]{1,0:T(8,128)} %rows_hbm.1), channel_id=1, source_target_pairs={{0,2},{1,3},{2,0},{3,1},{4,6},{5,7},{6,4},{7,5},{8,10},{9,11},{10,... | collective-permute-start | bytes 983048 | tf_op jit(solution)/shard_map/ppermute | solution.py:249
  4.0 11.4 %collective-permute-start.1 = (f32[320,128]{1,0:T(8,128)S(1)}, f32[320,128]{1,0:T(8,128)S(1)}, u32[]{:S(2)}, u32[]{:S(2)}) collective-permute-start(f32[320,128]{1,0:T(8,128)S(1)} %get-tuple-element.26.refs_1_), channel_id=1, source_target_pairs={{0,4},{1,5},{2,6},{3,7},{4,0},{5,1},{6,2},{7,3},{8,12},{9,13},{10,... | collective-permute-start | bytes 491528 | tf_op jit(solution)/shard_map/ppermute | solution.py:249
  6.7 15.3 %collective-permute-start.3 = (f32[320,128]{1,0:T(8,128)S(1)}, f32[320,128]{1,0:T(8,128)S(1)}, u32[]{:S(2)}, u32[]{:S(2)}) collective-permute-start(f32[320,128]{1,0:T(8,128)S(1)} %get-tuple-element.27.refs_2_), channel_id=1, source_target_pairs={{0,4},{1,5},{2,6},{3,7},{4,0},{5,1},{6,2},{7,3},{8,12},{9,13},{10,... | collective-permute-start | bytes 491528 | tf_op jit(solution)/shard_map/ppermute | solution.py:249
  15.4 9.0 %collective-permute-start.5 = (f32[320,128]{1,0:T(8,128)S(1)}, f32[320,128]{1,0:T(8,128)S(1)}, u32[]{:S(2)}, u32[]{:S(2)}) collective-permute-start(f32[320,128]{1,0:T(8,128)S(1)} %collective-permute-done.1.refs_1_), channel_id=1, source_target_pairs={{0,2},{1,3},{2,0},{3,1},{4,6},{5,7},{6,4},{7,5},{8,10},{9,11},{10,... | collective-permute-start | bytes 491528 | tf_op jit(solution)/shard_map/ppermute | solution.py:249
  18.4 1.4 %collective-permute-start.2 = (f32[320,128]{1,0:T(8,128)S(1)}, f32[320,128]{1,0:T(8,128)S(1)}, u32[]{:S(2)}, u32[]{:S(2)}) collective-permute-start(f32[320,128]{1,0:T(8,128)S(1)} %collective-permute-done.1.refs_1_), channel_id=1, source_target_pairs={{0,1},{1,0},{2,3},{3,2},{4,5},{5,4},{6,7},{7,6},{8,9},{9,8},{10,11... | collective-permute-start | bytes 491528 | tf_op jit(solution)/shard_map/ppermute | solution.py:249
  22.0 6.2 %collective-permute-start.9 = (f32[320,128]{1,0:T(8,128)S(1)}, f32[320,128]{1,0:T(8,128)S(1)}, u32[]{:S(2)}, u32[]{:S(2)}) collective-permute-start(f32[320,128]{1,0:T(8,128)S(1)} %collective-permute-done.3.refs_1_), channel_id=1, source_target_pairs={{0,2},{1,3},{2,0},{3,1},{4,6},{5,7},{6,4},{7,5},{8,10},{9,11},{10,... | collective-permute-start | bytes 491528 | tf_op jit(solution)/shard_map/ppermute | solution.py:249
  22.0 2.7 %collective-permute-start.7 = (f32[320,128]{1,0:T(8,128)S(1)}, f32[320,128]{1,0:T(8,128)S(1)}, u32[]{:S(2)}, u32[]{:S(2)}) collective-permute-start(f32[320,128]{1,0:T(8,128)S(1)} %collective-permute-done.3.refs_1_), channel_id=1, source_target_pairs={{0,1},{1,0},{2,3},{3,2},{4,5},{5,4},{6,7},{7,6},{8,9},{9,8},{10,11... | collective-permute-start | bytes 491528 | tf_op jit(solution)/shard_map/ppermute | solution.py:249
  22.2 2.5 %collective-permute-start.8 = (f32[640,128]{1,0:T(8,128)S(1)}, f32[640,128]{1,0:T(8,128)S(1)}, u32[]{:S(2)}, u32[]{:S(2)}) collective-permute-start(f32[640,128]{1,0:T(8,128)S(1)} %collective-permute-done.4.refs_2_), channel_id=1, source_target_pairs={{0,1},{1,0},{2,3},{3,2},{4,5},{5,4},{6,7},{7,6},{8,9},{9,8},{10,11... | collective-permute-start | bytes 983048 | tf_op jit(solution)/shard_map/ppermute | solution.py:249
  24.5 4.8 %collective-permute-start.6 = (f32[320,128]{1,0:T(8,128)S(1)}, f32[320,128]{1,0:T(8,128)S(1)}, u32[]{:S(2)}, u32[]{:S(2)}) collective-permute-start(f32[320,128]{1,0:T(8,128)S(1)} %collective-permute-done.5.refs_3_), channel_id=1, source_target_pairs={{0,1},{1,0},{2,3},{3,2},{4,5},{5,4},{6,7},{7,6},{8,9},{9,8},{10,11... | collective-permute-start | bytes 491528 | tf_op jit(solution)/shard_map/ppermute | solution.py:249
  28.2 1.4 %collective-permute-start.10 = (f32[320,128]{1,0:T(8,128)S(1)}, f32[320,128]{1,0:T(8,128)S(1)}, u32[]{:S(2)}, u32[]{:S(2)}) collective-permute-start(f32[320,128]{1,0:T(8,128)S(1)} %collective-permute-done.9.refs_1_), channel_id=1, source_target_pairs={{0,1},{1,0},{2,3},{3,2},{4,5},{5,4},{6,7},{7,6},{8,9},{9,8},{10,11... | collective-permute-start | bytes 491528 | tf_op jit(solution)/shard_map/ppermute | solution.py:249

commit v5 on v4

--- a/solution.py
+++ b/solution.py
@@ -279,12 +279,12 @@
     moving = [[], []]
     pending = halves[0] + halves[1] + near_own
     for bit, close in zip(bits[1:], direct):
-        state = computed(state, pending, now=True)
         state, first = after(state, fresh[0])
         moving[0] = moving[0] + first
         first_on = swapped(moving[0], bit)
+        state = fenced(state)
         near = swapped(first, 1)
-        state = fenced(state)
+        state = computed(state, pending, now=True)
         state = computed(state, first + near, now=True)
 
         state, second = after(state, fresh[1])

time: 31.9 us -> 32 us (level)
  transfers between devices with their start and end apart: 11 -> 11, of which waited for: 4 -> 3; matrix products, arithmetic and copies ran while one was open for 0% -> 0% of each run, Pallas kernels for 55% -> 51%
where the time goes in v5:
time: 32 us; the launch traced here: 31.8 us
  Pallas kernels  19.4 us (61%)
  starting transfers between devices  9.42 us (29%)
  waiting for transfers between devices  2.82 us (9%)
    pallas_call x6, Pallas kernels, update(): pl.pallas_call(functools.partial(update_kernel, places, before, now, bloc...  13.2 us
    ppermute x11, starting transfers between devices, swapped(): lax.ppermute(block, 'col', pairs)  9.42 us
    pallas_call x1, Pallas kernels, setup(): pl.pallas_call(setup_kernel, out_shape=(jax.ShapeDtypeStruct((4 * dim, 2...  5.19 us
    ppermute x11, waiting for transfers between devices, swapped(): lax.ppermute(block, 'col', pairs)  2.82 us
    pallas_call x1, Pallas kernels, parts(): pl.pallas_call(parts_kernel, out_shape=tuple((jax.ShapeDtypeStruct(shape,...  1.01 us
  transfers between devices with their start and end apart: 11, of which 3 were waited for; matrix products, arithmetic and copies ran while one was open for 0% of the time, Pallas kernels for 51%

profile of v5, /device:TPU:0, one launch (start us, length us, event | category | flops | bytes accessed | tf_op | source)
XLA Modules:
  0.0 31.8 jit_solution(7551229527657901512)
XLA Ops:
  0.0 1.0 %parts.1 = (f32[320,128]{1,0:T(8,128)S(1)}, f32[320,128]{1,0:T(8,128)S(1)}) custom-call(f32[640,128]{1,0:T(8,128)} %rows_hbm.1), custom_call_target="tpu_custom_call" | custom-call | bytes 1000000 | tf_op jit(solution)/shard_map/parts/pallas_call | solution.py:222
  1.0 4.1 %collective-permute-start = (f32[320,128]{1,0:T(8,128)S(1)}, f32[320,128]{1,0:T(8,128)S(1)}, u32[]{:S(2)}, u32[]{:S(2)}) collective-permute-start(f32[320,128]{1,0:T(8,128)S(1)} %get-tuple-element.27.refs_1_), channel_id=1, source_target_pairs={{0,4},{1,5},{2,6},{3,7},{4,0},{5,1},{6,2},{7,3},{8,12},{9,13},{10,... | collective-permute-start | bytes 491528 | tf_op jit(solution)/shard_map/ppermute | solution.py:249
  5.1 1.6 %collective-permute-start.4 = (f32[640,128]{1,0:T(8,128)}, f32[640,128]{1,0:T(8,128)S(1)}, u32[]{:S(2)}, u32[]{:S(2)}) collective-permute-start(f32[640,128]{1,0:T(8,128)} %rows_hbm.1), channel_id=1, source_target_pairs={{0,2},{1,3},{2,0},{3,1},{4,6},{5,7},{6,4},{7,5},{8,10},{9,11},{10,... | collective-permute-start | bytes 983048 | tf_op jit(solution)/shard_map/ppermute | solution.py:249
  6.7 0.0 collective-permute-start.2
  6.7 0.3 %collective-permute-start.3 = (f32[320,128]{1,0:T(8,128)S(1)}, f32[320,128]{1,0:T(8,128)S(1)}, u32[]{:S(2)}, u32[]{:S(2)}) collective-permute-start(f32[320,128]{1,0:T(8,128)S(1)} %get-tuple-element.31.refs_2_), channel_id=1, source_target_pairs={{0,4},{1,5},{2,6},{3,7},{4,0},{5,1},{6,2},{7,3},{8,12},{9,13},{10,... | collective-permute-start | bytes 491528 | tf_op jit(solution)/shard_map/ppermute | solution.py:249
  7.0 5.2 %setup.1 = (bf16[512,768]{1,0:T(8,128)(2,1)S(1)}, bf16[1536,256]{1,0:T(8,128)(2,1)S(1)}, f32[5120,256]{1,0:T(8,128)}) custom-call(f32[256,128]{1,0:T(8,128)} %slab_hbm.1, f32[2,256,128]{2,1,0:T(8,128)} %panel_hbm.1, f32[2,256,256]{2,1,0:T(8,128)} %inverse_hbm.1), custom_call_target="tpu_custom_call" | custom-call | flops 1700000000 | bytes 4194304 | tf_op jit(solution)/shard_map/setup/pallas_call | solution.py:88
  12.2 1.5 %collective-permute-done.refs_1_ = f32[320,128]{1,0:T(8,128)S(1)} collective-permute-done((f32[320,128]{1,0:T(8,128)S(1)}, f32[320,128]{1,0:T(8,128)S(1)}, u32[]{:S(2)}, u32[]{:S(2)}) %collective-permute-start) | collective-permute-done | bytes 163872 | tf_op jit(solution)/shard_map/ppermute | solution.py:249
  13.8 0.0 collective-permute-start.5
  13.8 0.0 collective-permute-start.1
  13.8 0.0 collective-permute-done.2.refs_3_
  13.8 3.2 %update.6.refs_5_ = f32[5120,256]{1,0:T(8,128)} custom-call(s32[1]{0:T(128)} %bitcast.refs_0_, f32[320,128]{1,0:T(8,128)S(1)} %get-tuple-element.27.refs_1_, f32[320,128]{1,0:T(8,128)S(1)} %get-tuple-element.31.refs_2_, f32[640,128]{1,0:T(8,128)S(1)} %collective-permute-done.2.refs_3_, ...), custom_call_target="tpu_custom_call", output_to_operand_aliasing={{}: (6, {})} | custom-call | flops 10000000000 | bytes 10000000 | tf_op jit(solution)/shard_map/update/pallas_call | solution.py:190
  17.0 2.1 %update.7.held_ref = f32[5120,256]{1,0:T(8,128)} custom-call(s32[1]{0:T(128)} %bitcast.refs_0_, f32[320,128]{1,0:T(8,128)S(1)} %collective-permute-done.refs_1_, f32[320,128]{1,0:T(8,128)S(1)} %collective-permute-done.1.refs_2_, bf16[512,768]{1,0:T(8,128)(2,1)S(1)} %get-tuple-element.29.refs_4_.refs_3_.refs_2_, ...), custom_call_target="tpu_custom_call", output_to_operand_aliasing={{}: (5, {})} | custom-call | flops 10000000000 | bytes 10000000 | tf_op jit(solution)/shard_map/update/pallas_call | solution.py:190
  19.1 1.2 %collective-permute-done.3.refs_1_ = f32[320,128]{1,0:T(8,128)S(1)} collective-permute-done((f32[320,128]{1,0:T(8,128)S(1)}, f32[320,128]{1,0:T(8,128)S(1)}, u32[]{:S(2)}, u32[]{:S(2)}) %collective-permute-start.3) | collective-permute-done | bytes 163872 | tf_op jit(solution)/shard_map/ppermute | solution.py:249
  20.3 2.3 %collective-permute-start.9 = (f32[320,128]{1,0:T(8,128)S(1)}, f32[320,128]{1,0:T(8,128)S(1)}, u32[]{:S(2)}, u32[]{:S(2)}) collective-permute-start(f32[320,128]{1,0:T(8,128)S(1)} %collective-permute-done.3.refs_1_), channel_id=1, source_target_pairs={{0,2},{1,3},{2,0},{3,1},{4,6},{5,7},{6,4},{7,5},{8,10},{9,11},{10,... | collective-permute-start | bytes 491528 | tf_op jit(solution)/shard_map/ppermute | solution.py:249
  22.6 0.0 collective-permute-done.4.refs_2_
  22.6 0.5 %collective-permute-start.8 = (f32[640,128]{1,0:T(8,128)S(1)}, f32[640,128]{1,0:T(8,128)S(1)}, u32[]{:S(2)}, u32[]{:S(2)}) collective-permute-start(f32[640,128]{1,0:T(8,128)S(1)} %collective-permute-done.4.refs_2_), channel_id=1, source_target_pairs={{0,1},{1,0},{2,3},{3,2},{4,5},{5,4},{6,7},{7,6},{8,9},{9,8},{10,11... | collective-permute-start | bytes 983048 | tf_op jit(solution)/shard_map/ppermute | solution.py:249
  23.1 1.9 %update.8 = (f32[5120,256]{1,0:T(8,128)}, f32[960,256]{1,0:T(8,128)S(1)}) custom-call(s32[1]{0:T(128)} %bitcast.refs_0_, f32[320,128]{1,0:T(8,128)S(1)} %collective-permute-done.3.refs_1_, f32[640,128]{1,0:T(8,128)S(1)} %collective-permute-done.4.refs_2_, ...), custom_call_target="tpu_custom_call", output_to_operand_aliasing={{0}: (5, {})} | custom-call | flops 10000000000 | bytes 10000000 | tf_op jit(solution)/shard_map/update/pallas_call | solution.py:190
  25.1 0.1 collective-permute-done.5.refs_3_
  25.1 0.0 collective-permute-start.6
  25.2 0.0 collective-permute-done.7.refs_1_
  25.2 2.8 %update.9 = (f32[5120,256]{1,0:T(8,128)}, f32[1280,256]{1,0:T(8,128)S(1)}) custom-call(s32[1]{0:T(128)} %bitcast.refs_0_, f32[320,128]{1,0:T(8,128)S(1)} %collective-permute-done.7.refs_1_, f32[640,128]{1,0:T(8,128)S(1)} %collective-permute-done.8.refs_2_, f32[320,128]{1,0:T(8,128)S(1)} %collective-permute-done.5.refs_3_, ...), custom_call_target="tpu_custom_call", output_to_operand_aliasing={{0}: (7, {})} | custom-call | flops 10000000000 | bytes 10000000 | tf_op jit(solution)/shard_map/update/pallas_call | solution.py:190
  28.0 0.5 %collective-permute-start.10 = (f32[320,128]{1,0:T(8,128)S(1)}, f32[320,128]{1,0:T(8,128)S(1)}, u32[]{:S(2)}, u32[]{:S(2)}) collective-permute-start(f32[320,128]{1,0:T(8,128)S(1)} %collective-permute-done.9.refs_1_), channel_id=1, source_target_pairs={{0,1},{1,0},{2,3},{3,2},{4,5},{5,4},{6,7},{7,6},{8,9},{9,8},{10,11... | collective-permute-start | bytes 491528 | tf_op jit(solution)/shard_map/ppermute | solution.py:249
  28.6 1.1 %update.10 = (f32[5120,256]{1,0:T(8,128)}, f32[320,256]{1,0:T(8,128)S(1)}) custom-call(s32[1]{0:T(128)} %bitcast.refs_0_, f32[320,128]{1,0:T(8,128)S(1)} %collective-permute-done.9.refs_1_, bf16[512,768]{1,0:T(8,128)(2,1)S(1)} %get-tuple-element.29.refs_4_.refs_3_.refs_2_, ...), custom_call_target="tpu_custom_call", output_to_operand_aliasing={{0}: (5, {})} | custom-call | flops 10000000000 | bytes 10000000 | tf_op jit(solution)/shard_map/update/pallas_call | solution.py:190
  29.7 2.1 %update.11 = f32[5120,256]{1,0:T(8,128)} custom-call(s32[1]{0:T(128)} %bitcast.refs_0_, f32[320,128]{1,0:T(8,128)S(1)} %collective-permute-done.6.refs_1_, f32[320,128]{1,0:T(8,128)S(1)} %collective-permute-done.10.refs_2_, bf16[512,768]{1,0:T(8,128)(2,1)S(1)} %get-tuple-element.29.refs_4_.refs_3_.refs_2_, ...), custom_call_target="tpu_custom_call", output_to_operand_aliasing={{}: (6, {})} | custom-call | flops 10000000000 | bytes 10000000 | tf_op jit(solution)/shard_map/update/pallas_call | solution.py:190
  (8 shorter events, 0.0 us)
Async XLA Ops:
  1.0 12.7 %collective-permute-start = (f32[320,128]{1,0:T(8,128)S(1)}, f32[320,128]{1,0:T(8,128)S(1)}, u32[]{:S(2)}, u32[]{:S(2)}) collective-permute-start(f32[320,128]{1,0:T(8,128)S(1)} %get-tuple-element.27.refs_1_), channel_id=1, source_target_pairs={{0,4},{1,5},{2,6},{3,7},{4,0},{5,1},{6,2},{7,3},{8,12},{9,13},{10,... | collective-permute-start | bytes 491528 | tf_op jit(solution)/shard_map/ppermute | solution.py:249
  5.1 17.5 %collective-permute-start.4 = (f32[640,128]{1,0:T(8,128)}, f32[640,128]{1,0:T(8,128)S(1)}, u32[]{:S(2)}, u32[]{:S(2)}) collective-permute-start(f32[640,128]{1,0:T(8,128)} %rows_hbm.1), channel_id=1, source_target_pairs={{0,2},{1,3},{2,0},{3,1},{4,6},{5,7},{6,4},{7,5},{8,10},{9,11},{10,... | collective-permute-start | bytes 983048 | tf_op jit(solution)/shard_map/ppermute | solution.py:249
  6.7 7.1 %collective-permute-start.2 = (f32[640,128]{1,0:T(8,128)}, f32[640,128]{1,0:T(8,128)S(1)}, u32[]{:S(2)}, u32[]{:S(2)}) collective-permute-start(f32[640,128]{1,0:T(8,128)} %rows_hbm.1), channel_id=1, source_target_pairs={{0,1},{1,0},{2,3},{3,2},{4,5},{5,4},{6,7},{7,6},{8,9},{9,8},{10,11... | collective-permute-start | bytes 983048 | tf_op jit(solution)/shard_map/ppermute | solution.py:249
  6.7 13.6 %collective-permute-start.3 = (f32[320,128]{1,0:T(8,128)S(1)}, f32[320,128]{1,0:T(8,128)S(1)}, u32[]{:S(2)}, u32[]{:S(2)}) collective-permute-start(f32[320,128]{1,0:T(8,128)S(1)} %get-tuple-element.31.refs_2_), channel_id=1, source_target_pairs={{0,4},{1,5},{2,6},{3,7},{4,0},{5,1},{6,2},{7,3},{8,12},{9,13},{10,... | collective-permute-start | bytes 491528 | tf_op jit(solution)/shard_map/ppermute | solution.py:249
  13.8 11.4 %collective-permute-start.5 = (f32[320,128]{1,0:T(8,128)S(1)}, f32[320,128]{1,0:T(8,128)S(1)}, u32[]{:S(2)}, u32[]{:S(2)}) collective-permute-start(f32[320,128]{1,0:T(8,128)S(1)} %collective-permute-done.refs_1_), channel_id=1, source_target_pairs={{0,2},{1,3},{2,0},{3,1},{4,6},{5,7},{6,4},{7,5},{8,10},{9,11},{10,... | collective-permute-start | bytes 491528 | tf_op jit(solution)/shard_map/ppermute | solution.py:249
  13.8 3.2 %collective-permute-start.1 = (f32[320,128]{1,0:T(8,128)S(1)}, f32[320,128]{1,0:T(8,128)S(1)}, u32[]{:S(2)}, u32[]{:S(2)}) collective-permute-start(f32[320,128]{1,0:T(8,128)S(1)} %collective-permute-done.refs_1_), channel_id=1, source_target_pairs={{0,1},{1,0},{2,3},{3,2},{4,5},{5,4},{6,7},{7,6},{8,9},{9,8},{10,11... | collective-permute-start | bytes 491528 | tf_op jit(solution)/shard_map/ppermute | solution.py:249
  20.3 7.7 %collective-permute-start.9 = (f32[320,128]{1,0:T(8,128)S(1)}, f32[320,128]{1,0:T(8,128)S(1)}, u32[]{:S(2)}, u32[]{:S(2)}) collective-permute-start(f32[320,128]{1,0:T(8,128)S(1)} %collective-permute-done.3.refs_1_), channel_id=1, source_target_pairs={{0,2},{1,3},{2,0},{3,1},{4,6},{5,7},{6,4},{7,5},{8,10},{9,11},{10,... | collective-permute-start | bytes 491528 | tf_op jit(solution)/shard_map/ppermute | solution.py:249
  22.6 2.5 %collective-permute-start.7 = (f32[320,128]{1,0:T(8,128)S(1)}, f32[320,128]{1,0:T(8,128)S(1)}, u32[]{:S(2)}, u32[]{:S(2)}) collective-permute-start(f32[320,128]{1,0:T(8,128)S(1)} %collective-permute-done.3.refs_1_), channel_id=1, source_target_pairs={{0,1},{1,0},{2,3},{3,2},{4,5},{5,4},{6,7},{7,6},{8,9},{9,8},{10,11... | collective-permute-start | bytes 491528 | tf_op jit(solution)/shard_map/ppermute | solution.py:249
  22.6 2.5 %collective-permute-start.8 = (f32[640,128]{1,0:T(8,128)S(1)}, f32[640,128]{1,0:T(8,128)S(1)}, u32[]{:S(2)}, u32[]{:S(2)}) collective-permute-start(f32[640,128]{1,0:T(8,128)S(1)} %collective-permute-done.4.refs_2_), channel_id=1, source_target_pairs={{0,1},{1,0},{2,3},{3,2},{4,5},{5,4},{6,7},{7,6},{8,9},{9,8},{10,11... | collective-permute-start | bytes 983048 | tf_op jit(solution)/shard_map/ppermute | solution.py:249
  25.1 4.5 %collective-permute-start.6 = (f32[320,128]{1,0:T(8,128)S(1)}, f32[320,128]{1,0:T(8,128)S(1)}, u32[]{:S(2)}, u32[]{:S(2)}) collective-permute-start(f32[320,128]{1,0:T(8,128)S(1)} %collective-permute-done.5.refs_3_), channel_id=1, source_target_pairs={{0,1},{1,0},{2,3},{3,2},{4,5},{5,4},{6,7},{7,6},{8,9},{9,8},{10,11... | collective-permute-start | bytes 491528 | tf_op jit(solution)/shard_map/ppermute | solution.py:249
  28.0 1.7 %collective-permute-start.10 = (f32[320,128]{1,0:T(8,128)S(1)}, f32[320,128]{1,0:T(8,128)S(1)}, u32[]{:S(2)}, u32[]{:S(2)}) collective-permute-start(f32[320,128]{1,0:T(8,128)S(1)} %collective-permute-done.9.refs_1_), channel_id=1, source_target_pairs={{0,1},{1,0},{2,3},{3,2},{4,5},{5,4},{6,7},{7,6},{8,9},{9,8},{10,11... | collective-permute-start | bytes 491528 | tf_op jit(solution)/shard_map/ppermute | solution.py:249
